TPU v7x, 256 devices: a whole 4x4x8 slice. The times are simulated.
256 devices in a mesh: dp: 32 (over x_hi, z, core), mp: 8 (over y, x_lo).
Axes of the slice: x: 4 (x_hi: 2, x_lo: 2; x = x_hi * 2 + x_lo), y: 4, z: 8, core: 2. Of those that a mesh axis runs over, the one named last changes fastest.
Arguments:
- acts: bfloat16 [32768, 8192], P('dp', 'mp'), may hold values from -6 to 6
- cotangent: bfloat16 [32768, 8, 256], P('dp', 'mp'), may hold values from -0.03125 to 0.03125
- master: float32 [8192, 8, 256], P('dp', 'mp'), may hold values from -0.0625 to 0.0625
- first_moment: float32 [8192, 8, 256], P('dp', 'mp'), may hold values from -6 to 6
- second_moment: float32 [8192, 8, 256], P('dp', 'mp'), may hold values from 0.25 to 4
- long_acts: bfloat16 [8192, 8192], P('dp'), may hold values from -6 to 6
Outputs:
- new_master: float32 [8192, 8, 256], P(('dp', 'mp'))
- new_first: float32 [8192, 8, 256], P(('dp', 'mp'))
- new_second: float32 [8192, 8, 256], P(('dp', 'mp'))
- long_kv: bfloat16 [8192, 8, 256], P('dp', 'mp')
All inputs are finite; a program needn't handle non-finite values.
Results may differ from a plain program's by a relative error of at most 0.005.
Values may be sent and summed in bfloat16 or wider, within the bound.
A program may use at most 128 MiB of HBM per device.

v0:
```python
import jax
import jax.numpy as jnp
from jax import lax
from jax.sharding import PartitionSpec as P

beta_one = 0.9
beta_two = 0.95
learn_rate = 0.001
decay_rate = 0.1
adam_eps = 1e-08
steps_done = 100


def on_device(acts, cotangent, master, first_moment, second_moment, long_acts):
    gathered = lax.all_gather(acts, "mp", axis=1, tiled=True)
    flat_cot = cotangent.reshape(cotangent.shape[0], -1)
    columns = gathered
    product = lax.dot_general(
        columns, flat_cot, (((0,), (0,)), ((), ())), preferred_element_type=jnp.float32
    )
    grad = lax.psum_scatter(
        product.reshape(
            lax.axis_size("dp") * master.shape[0], master.shape[1], master.shape[2]
        ).astype(jnp.bfloat16),
        "dp",
        scatter_dimension=0,
        tiled=True,
    ).astype(jnp.float32)
    first_next = beta_one * first_moment + (1.0 - beta_one) * grad
    second_next = beta_two * second_moment + (1.0 - beta_two) * grad * grad
    fix_one = 1.0 - beta_one**steps_done
    fix_two = 1.0 - beta_two**steps_done
    update = (
        first_next / fix_one / (jnp.sqrt(second_next / fix_two) + adam_eps) + decay_rate * master
    )
    master_next = master - learn_rate * update
    new_master, new_first, new_second = (
        lax.all_to_all(master_next, "mp", split_axis=0, concat_axis=1, tiled=True),
        lax.all_to_all(first_next, "mp", split_axis=0, concat_axis=1, tiled=True),
        lax.all_to_all(second_next, "mp", split_axis=0, concat_axis=1, tiled=True),
    )
    weights = new_master.astype(jnp.bfloat16)
    long_rows = long_acts.shape[0]
    split_acts = long_acts.reshape(long_rows, lax.axis_size("dp"), lax.axis_size("mp"), -1)
    stripe = lax.dynamic_index_in_dim(split_acts, lax.axis_index("mp"), 2, keepdims=False).reshape(
        long_rows, -1
    )
    piece = lax.all_gather(weights, "dp", axis=0, tiled=True)
    columns = stripe
    partial_kv = jnp.dot(
        columns, piece.reshape(piece.shape[0], -1), preferred_element_type=jnp.float32
    )
    partial_kv = partial_kv.reshape(long_rows, weights.shape[1], weights.shape[2])
    long_kv = lax.psum_scatter(partial_kv, "mp", scatter_dimension=1, tiled=True).astype(
        jnp.bfloat16
    )
    return (new_master, new_first, new_second, long_kv)


def solution(mesh):
    in_specs = (
        P("dp", "mp"),
        P("dp", "mp", None),
        P("dp", "mp", None),
        P("dp", "mp", None),
        P("dp", "mp", None),
        P("dp", None),
    )
    out_specs = (
        P(("dp", "mp"), None, None),
        P(("dp", "mp"), None, None),
        P(("dp", "mp"), None, None),
        P("dp", "mp", None),
    )
    return jax.shard_map(
        on_device, mesh=mesh, in_specs=in_specs, out_specs=out_specs, check_vma=False
    )
```

profile of v0, /device:TPU:1, one launch (start us, length us, event | category | flops | bytes accessed | tf_op | source)
XLA Modules:
  0.0 656.2 jit_solution(6705560739923045763)
XLA Ops:
  7.2 0.0 copy-start
  7.2 0.0 all-gather.3.cloned.1.call-start
  7.2 0.7 all-gather.3.cloned.1.call-update
  7.9 0.0 reduce-scatter.3.cloned.1.call-start
  8.0 333.8 %all-gather.3.cloned.1.call-done = bf16[1024,8192]{1,0:T(8,128)(2,1)} async-done(((bf16[1024,1024]{1,0:T(8,128)(2,1)}), bf16[1024,8192]{1,0:T(8,128)(2,1)}) %all-gather.3.cloned.1.call-update) | async-done | bytes 16777232 | tf_op jit(solution)/shard_map/all_gather | solution.py:15
  341.8 0.0 copy-done
  341.8 12.5 %fusion = bf16[8192,1,256]{2,0,1:T(8,128)(2,1)} fusion(bf16[1024,8192]{1,0:T(8,128)(2,1)} %all-gather.3.cloned.1.call-done, bf16[1024,1,256]{2,0,1:T(8,128)(2,1)S(1)} %copy-done), kind=kOutput, calls=%fused_computation.1 | convolution fusion | flops 4297064448 | bytes 21495808 | tf_op jit(solution)/shard_map/dot_general | solution.py:18
  354.4 0.0 copy-start.1
  354.4 0.0 copy-start.2
  354.4 0.0 copy-start.3
  354.4 0.0 reduce-scatter.3.cloned.1.call-update
  354.4 0.0 all-gather.5.cloned.1.call-start
  354.4 124.1 %reduce-scatter.3.cloned.1.call-done = bf16[256,1,256]{2,0,1:T(8,128)(2,1)} async-done(((bf16[8192,1,256]{2,0,1:T(8,128)(2,1)}), bf16[256,1,256]{2,0,1:T(8,128)(2,1)}) %reduce-scatter.3.cloned.1.call-update) | async-done | bytes 131088 | tf_op jit(solution)/shard_map/reduce_scatter | solution.py:21
  478.5 0.0 copy-done.1
  478.5 0.0 copy-done.2
  478.5 0.0 copy-done.3
  478.5 1.1 multiply_subtract_fusion
  479.7 0.3 copy.33
  479.9 10.3 %all_to_all.54 = f32[256,1,256]{2,1,0:T(1,128)S(1)} all-to-all(f32[256,1,256]{2,1,0:T(1,128)S(1)} %copy.33), channel_id=1, replica_groups=mesh['dp'=32,'mp'=8] {'mp'}, dimensions={0} | all-to-all | bytes 524288 | tf_op jit(solution)/shard_map/all_to_all | solution.py:38
  490.2 0.9 fusion.6
  491.1 0.0 all-gather.5.cloned.1.call-update
  491.2 0.0 reduce-scatter.5.cloned.1.call-start
  491.2 6.5 copy.39
  497.7 1.1 constant_dynamic-slice_fusion
  498.8 82.5 %all-gather.5.cloned.1.call-done = bf16[1024,8,256]{2,1,0:T(8,128)(2,1)} async-done(((bf16[32,8,256]{2,1,0:T(8,128)(2,1)}), bf16[1024,8,256]{2,1,0:T(8,128)(2,1)}) %all-gather.5.cloned.1.call-update) | async-done | bytes 4194320 | tf_op jit(solution)/shard_map/all_gather | solution.py:48
  581.2 6.7 %copy.44 = bf16[1024,8,256]{0,2,1:T(8,128)(2,1)} copy(bf16[1024,8,256]{2,1,0:T(8,128)(2,1)} %all-gather.5.cloned.1.call-done) | data formatting | bytes 8388608 | tf_op jit(solution)/shard_map/reshape | solution.py:51
  588.0 4.8 fusion.1
  592.8 0.0 reduce-scatter.5.cloned.1.call-update
  592.8 1.0 copy.35
  593.8 4.0 all-to-all-start.1
  597.8 1.0 copy.37
  598.8 5.6 all-to-all-done.1
  604.4 3.4 all-to-all-start.2
  607.8 0.9 copy.59
  608.6 8.6 %all-to-all-done.2 = f32[256,1,256]{2,1,0:T(1,128)S(1)} async-done(((f32[256,1,256]{2,1,0:T(1,128)}), f32[256,1,256]{2,1,0:T(1,128)S(1)}, u32[]{:S(2)}, u32[]{:S(2)}) %all-to-all-start.2) | async-done | bytes 262176 | tf_op jit(solution)/shard_map/all_to_all | solution.py:40
  617.3 0.9 copy.58
  618.1 29.9 %reduce-scatter.5.cloned.1.call-done = f32[256,1,256]{2,0,1:T(8,128)} async-done(((f32[256,8,256]{2,0,1:T(8,128)}), f32[256,1,256]{2,0,1:T(8,128)}) %reduce-scatter.5.cloned.1.call-update) | async-done | bytes 262160 | tf_op jit(solution)/shard_map/reduce_scatter | solution.py:54
  648.0 1.6 convert_element_type.19
Async XLA Ops:
  7.2 334.6 %copy-start = (bf16[1024,1,256]{2,0,1:T(8,128)(2,1)S(1)}, bf16[1024,1,256]{2,0,1:T(8,128)(2,1)}, u32[]{:S(2)}) copy-start(bf16[1024,1,256]{2,0,1:T(8,128)(2,1)} %param.7) | copy-start | bytes 1572868
  7.2 334.6 %all-gather.3.cloned.1.call-start = ((), (), s32[]{:S(2)}) async-start(), calls=%async_computation.5 | async-start | bytes 18874368 | tf_op jit(solution)/shard_map/all_gather | solution.py:15
  7.9 470.6 %reduce-scatter.3.cloned.1.call-start = ((), (), s32[]{:S(2)}) async-start(), calls=%async_computation.6 | async-start | bytes 4325376 | tf_op jit(solution)/shard_map/reduce_scatter | solution.py:21
  354.4 124.2 %copy-start.1 = (f32[256,1,256]{2,1,0:T(1,128)S(1)}, f32[256,1,256]{2,1,0:T(1,128)}, u32[]{:S(2)}) copy-start(f32[256,1,256]{2,1,0:T(1,128)} %param.8) | copy-start | bytes 786436
  354.4 124.2 %copy-start.2 = (f32[256,1,256]{2,1,0:T(1,128)S(1)}, f32[256,1,256]{2,1,0:T(1,128)}, u32[]{:S(2)}) copy-start(f32[256,1,256]{2,1,0:T(1,128)} %param.9) | copy-start | bytes 786436
  354.4 124.2 %copy-start.3 = (f32[256,1,256]{2,1,0:T(1,128)S(1)}, f32[256,1,256]{2,1,0:T(1,128)}, u32[]{:S(2)}) copy-start(f32[256,1,256]{2,1,0:T(1,128)} %param.10) | copy-start | bytes 786436
  354.4 226.9 %all-gather.5.cloned.1.call-start = ((), (), s32[]{:S(2)}) async-start(), calls=%async_computation.7 | async-start | bytes 4325376 | tf_op jit(solution)/shard_map/all_gather | solution.py:48
  491.2 156.8 %reduce-scatter.5.cloned.1.call-start = ((), (), s32[]{:S(2)}) async-start(), calls=%async_computation.8 | async-start | bytes 2359296 | tf_op jit(solution)/shard_map/reduce_scatter | solution.py:54
  593.8 10.6 %all-to-all-start.1 = ((f32[256,1,256]{2,1,0:T(1,128)}), f32[256,1,256]{2,1,0:T(1,128)S(1)}, u32[]{:S(2)}, u32[]{:S(2)}) async-start(f32[256,1,256]{2,1,0:T(1,128)} %copy.35), calls=%async_computation.2 | async-start | bytes 524288 | tf_op jit(solution)/shard_map/all_to_all | solution.py:39
  604.4 12.9 %all-to-all-start.2 = ((f32[256,1,256]{2,1,0:T(1,128)}), f32[256,1,256]{2,1,0:T(1,128)S(1)}, u32[]{:S(2)}, u32[]{:S(2)}) async-start(f32[256,1,256]{2,1,0:T(1,128)} %copy.37), calls=%async_computation.3 | async-start | bytes 524288 | tf_op jit(solution)/shard_map/all_to_all | solution.py:40
Sparse Core Ops, SparseCore 0:
  9.8 331.9 all-gather.2
  354.5 123.9 reduce-scatter.2
  491.3 89.9 all-gather.4
  592.9 55.0 reduce-scatter.4
where the time goes:
time: 657 us; the launch traced here: 656 us
  waiting for transfers between devices  585 us (89%)
  local copies, waits for them, and re-layouts  18.2 us (3%)
  matrix products  17.4 us (3%)
  between operations  13.8 us (2%)
  blocking collectives  10.3 us (2%)
  starting transfers between devices  7.59 us (1%)
    all_gather x1, waiting for transfers between devices, on_device(): gathered = lax.all_gather(acts, 'mp', axis=1, tiled=True)  334 us
    reduce_scatter x1, waiting for transfers between devices, on_device(): lax.psum_scatter(product.reshape(lax.axis_size('dp') * master.shape[0], m...  124 us
    all_gather x1, waiting for transfers between devices, on_device(): piece = lax.all_gather(weights, 'dp', axis=0, tiled=True)  82.5 us
    reduce_scatter x1, waiting for transfers between devices, on_device(): lax.psum_scatter(partial_kv, 'mp', scatter_dimension=1, tiled=True)  29.9 us
  transfers between devices with their start and end apart: 6, of which 6 were waited for; matrix products, arithmetic and copies ran while one was open for 2% of the time, Pallas kernels for 0%

commit v1 on v0

v1 whole, which is shorter than its diff:
```python
import jax
import jax.numpy as jnp
from jax import lax
from jax.experimental import pallas as pl
from jax.experimental.pallas import tpu as pltpu
from jax.sharding import PartitionSpec as P

beta_one = 0.9
beta_two = 0.95
learn_rate = 0.001
decay_rate = 0.1
adam_eps = 1e-08
steps_done = 100
fix_one = 1.0 - beta_one**steps_done
fix_two = 1.0 - beta_two**steps_done

F32, BF16 = jnp.float32, jnp.bfloat16
NZ = 8
NM = 8
ND = 32
FEAT = 1024
TOK = 1024
COL = 256
HALF = FEAT // 2
CH = HALF // NZ
ROWS = 256


def dp_index(xh, z, k):
    return xh * 16 + z * 2 + k


def mp_index(y, xl):
    return y * 2 + xl


def remote(src, dst, send_sem, recv_sem, dev):
    return pltpu.make_async_remote_copy(
        src_ref=src,
        dst_ref=dst,
        send_sem=send_sem,
        recv_sem=recv_sem,
        device_id=dev,
        device_id_type=pl.DeviceIdType.MESH,
    )


def kernel(
    acts_hbm, cot_hbm, mas_hbm, fir_hbm, sec_hbm, long_hbm,
    nm_ref, nf_ref, ns_ref, kv_ref,
    acts_v, acts_t, cots, prod, pair_out, pair_in, ring_out, ring_in, fin, land,
    state, fresh, arrived, w_all, long_v, acc,
    load_sem, cot_send, cot_recv, pair_send, pair_recv, ring_send, ring_recv,
    fin_send, land_recv, st_send, st_recv, x_sem, wr_send, wr_recv, sib_send, sib_recv,
):
    d, m = lax.axis_index("dp"), lax.axis_index("mp")
    xh, z, k = d // 16, (d // 2) % NZ, d % 2
    y, xl = m // 2, m % 2
    up, down = (z + 1) % NZ, (z + NZ - 1) % NZ
    yp, ym, yo = (y + 1) % 4, (y + 3) % 4, (y + 2) % 4
    xn = (d, mp_index(y, 1 - xl))
    dev_yp, dev_ym = (d, mp_index(yp, xl)), (d, mp_index(ym, xl))
    sib = (dp_index(xh, z, 1 - k), m)
    dev_up, dev_down = (dp_index(xh, up, k), m), (dp_index(xh, down, k), m)
    xpart = (dp_index(1 - xh, z, k), m)
    dt = dp_index(m // 4, 2 * (m % 4) + k, z // 4)
    src_m, src_k, src_z = d // 4, z % 2, k * 4

    loads = [
        pltpu.make_async_copy(cot_hbm, cots.at[m], load_sem.at[0]),
        pltpu.make_async_copy(acts_hbm, acts_v, load_sem.at[1]),
        pltpu.make_async_copy(mas_hbm, state.at[0], load_sem.at[2]),
        pltpu.make_async_copy(fir_hbm, state.at[1], load_sem.at[3]),
        pltpu.make_async_copy(sec_hbm, state.at[2], load_sem.at[4]),
        pltpu.make_async_copy(long_hbm, long_v, load_sem.at[5]),
    ]
    for load in loads:
        load.start()

    barrier = pltpu.get_barrier_semaphore()

    def greet(dev):
        pl.semaphore_signal(barrier, inc=1, device_id=dev, device_id_type=pl.DeviceIdType.MESH)

    for dev in (sib, dev_up, dev_down, xpart):
        greet(dev)
    for o in range(1, NM):
        greet((d, (m + o) % NM))
    for o in range(NM):
        greet((dt, (m + o) % NM))
    for a in range(2):
        for s in range(4):
            greet((dp_index(a, src_z + s, src_k), src_m))
    pl.semaphore_wait(barrier, 4 + NM - 1 + NM + 8)

    sends = []

    def go(copy):
        copy.start()
        sends.append(copy)
        return copy

    head = [
        m, mp_index(y, 1 - xl), mp_index(ym, xl), mp_index(yp, xl),
        mp_index(yo, xl), mp_index(ym, 1 - xl), mp_index(yp, 1 - xl), mp_index(yo, 1 - xl),
    ]
    low, high = pl.ds(0, TOK // 2), pl.ds(TOK // 2, TOK // 2)

    def cot_copy(n, block, dev):
        return remote(block, block, cot_send.at[n], cot_recv.at[n], dev)

    def cot_arrived(n, block):
        cot_copy(n, block, xn).wait_recv()

    def product(j):
        def tile(i, carry):
            rows = pl.multiple_of((1 - k) * HALF + i * 256, 256)
            pair_out[j, pl.ds(pl.multiple_of(i * 256, 256), 256), :] = jnp.dot(
                acts_t[pl.ds(rows, 256), :], cots[head[j]], preferred_element_type=F32
            ).astype(BF16)
            return carry

        lax.fori_loop(0, HALF // 256, tile, 0)
        go(remote(pair_out.at[j], pair_in.at[j], pair_send.at[j], pair_recv.at[j], sib))

        def mine(i, carry):
            rows = pl.multiple_of(k * HALF + i * 256, 256)
            prod[j, pl.ds(pl.multiple_of(i * 256, 256), 256), :] = jnp.dot(
                acts_t[pl.ds(rows, 256), :], cots[head[j]], preferred_element_type=F32
            )
            return carry

        lax.fori_loop(0, HALF // 256, mine, 0)

    def pair_arrived(j):
        remote(pair_out.at[j], pair_in.at[j], pair_send.at[j], pair_recv.at[j], sib).wait_recv()

    def ring_copy(g, r, s):
        return remote(
            ring_out.at[g, r, s], ring_in.at[g, r, s], ring_send.at[g, r, s], ring_recv.at[g, r, s],
            (dev_up, dev_down)[r],
        )

    def ring(g, s):
        for r in range(2):
            first = 4 * g + 2 * r
            chunk = (z + 2 * NZ - 1 - s) % NZ if r == 0 else (z + 1 + s) % NZ
            rows = pl.ds(pl.multiple_of(chunk * CH, CH), CH)
            total = prod[pl.ds(first, 2), rows, :] + pair_in[pl.ds(first, 2), rows, :].astype(F32)
            if s > 0:
                ring_copy(g, r, s - 1).wait_recv()
                total = total + ring_in[g, r, s - 1].astype(F32)
            if s < NZ - 1:
                ring_out[g, r, s] = total.astype(BF16)
                go(ring_copy(g, r, s))
            else:
                fin[pl.ds(first, 2)] = total.astype(BF16)
                for j in (first, first + 1):
                    hand_over(j)

    def final_copy(j):
        return remote(
            fin.at[j], land.at[xh, z % 4], fin_send.at[j], land_recv.at[xh, z % 4], (dt, head[j])
        )

    own_final = dt == d

    def hand_over(j):
        if j > 0:
            go(final_copy(j))
        else:

            @pl.when(own_final)
            def _():
                pltpu.make_async_copy(fin.at[0], land.at[xh, z % 4], land_recv.at[xh, z % 4]).start()

            @pl.when(jnp.logical_not(own_final))
            def _():
                final_copy(0).start()

    loads[0].wait()
    own = cots.at[m]
    go(cot_copy(0, own, xn))
    go(cot_copy(1, own, dev_yp))
    go(cot_copy(2, own, dev_ym))
    loads[1].wait()

    def turn(i, carry):
        rows = pl.ds(pl.multiple_of(i * 256, 256), 256)
        acts_t[rows, :] = acts_v[:, rows].T
        return carry

    lax.fori_loop(0, FEAT // 256, turn, 0)
    product(0)
    cot_arrived(1, cots.at[head[2]])
    go(cot_copy(3, cots.at[head[2], low], dev_yp))
    cot_arrived(2, cots.at[head[3]])
    go(cot_copy(4, cots.at[head[3], high], dev_ym))
    cot_arrived(0, cots.at[head[1]])
    go(cot_copy(5, cots.at[head[1]], dev_yp))
    go(cot_copy(6, cots.at[head[1]], dev_ym))
    for j in (1, 2, 3):
        product(j)
    for j in range(4):
        pair_arrived(j)
    ring(0, 0)
    cot_arrived(3, cots.at[head[4], low])
    go(cot_copy(7, cots.at[head[4], low], xn))
    cot_arrived(4, cots.at[head[4], high])
    go(cot_copy(8, cots.at[head[4], high], xn))
    product(4)
    ring(0, 1)
    ring(0, 2)
    cot_arrived(5, cots.at[head[5]])
    cot_arrived(6, cots.at[head[6]])
    product(5)
    product(6)
    ring(0, 3)
    cot_arrived(7, cots.at[head[7], low])
    cot_arrived(8, cots.at[head[7], high])
    product(7)
    for j in range(4, 8):
        pair_arrived(j)
    ring(1, 0)
    ring(0, 4)
    ring(1, 1)
    ring(0, 5)
    ring(1, 2)
    ring(0, 6)
    ring(1, 3)
    ring(0, 7)
    for s in range(4, NZ):
        ring(1, s)

    for n in (2, 3, 4):
        loads[n].wait()
    part = ROWS // 4
    for s in range(4):
        for a in range(2):
            remote(
                fin.at[0], land.at[a, s], fin_send.at[0], land_recv.at[a, s], xn
            ).wait_recv()
        rows = pl.ds(s * part, part)
        grad = land[0, s].astype(F32) + land[1, s].astype(F32)
        master, first, second = state[0, rows, :], state[1, rows, :], state[2, rows, :]
        first_next = beta_one * first + (1.0 - beta_one) * grad
        second_next = beta_two * second + (1.0 - beta_two) * grad * grad
        update = (
            first_next / fix_one / (jnp.sqrt(second_next / fix_two) + adam_eps)
            + decay_rate * master
        )
        master_next = master - learn_rate * update
        w_all[d, rows, :] = master_next.astype(BF16)
        for n, value in enumerate((master_next, first_next, second_next)):
            fresh[2 * s, n] = value[: part // 2]
            fresh[2 * s + 1, n] = value[part // 2 :]

    w_own = w_all.at[d]
    to_x = go(remote(w_own, w_own, x_sem.at[0], x_sem.at[1], xpart))
    top, bottom = pl.ds(0, ROWS // 2), pl.ds(ROWS // 2, ROWS // 2)

    def block_of(stream, r, s):
        at = (z + NZ - 1 - s) % NZ if r == 0 else (z + 1 + s) % NZ
        return dp_index(xh if stream == 0 else 1 - xh, at, k)

    def view(index, r, s):
        if s < 3:
            return w_all.at[index]
        return w_all.at[index, top if r == 0 else bottom]

    def weights_copy(stream, r, s):
        index = block_of(stream, r, s - 1) if s > 0 else dp_index(
            xh if stream == 0 else 1 - xh, z, k
        )
        src = view(index, r, s)
        return remote(
            src, src, wr_send.at[stream, r, s], wr_recv.at[stream, r, s], (dev_up, dev_down)[r]
        )

    def weights_arrived(stream, r, s):
        dst = view(block_of(stream, r, s), r, s)
        remote(
            dst, dst, wr_send.at[stream, r, s], wr_recv.at[stream, r, s], (dev_up, dev_down)[r]
        ).wait_recv()

    def to_sib(n, ref):
        go(remote(ref, ref, sib_send.at[n], sib_recv.at[n], sib))

    def sib_arrived(n, ref):
        remote(ref, ref, sib_send.at[n], sib_recv.at[n], sib).wait_recv()

    for r in range(2):
        go(weights_copy(0, r, 0))
    to_sib(0, w_own)

    def state_copy(o):
        to = (m + o) % NM
        return remote(fresh.at[to], arrived.at[m], st_send.at[o], st_recv.at[o], (d, to))

    for o in range(1, NM):
        go(state_copy(o))

    loads[5].wait()

    def add(index, start=False):
        cols = pl.ds(pl.multiple_of(index * ROWS, ROWS), ROWS)
        value = jnp.dot(long_v[:, cols], w_all[index], preferred_element_type=F32)
        if start:
            acc[...] = value
        else:
            acc[...] += value

    def other(index):
        return index + 1 - 2 * k

    add(d, True)
    sib_arrived(0, w_all.at[other(d)])
    add(other(d))
    across = dp_index(1 - xh, z, k)
    remote(w_all.at[across], w_all.at[across], x_sem.at[0], x_sem.at[1], xpart).wait_recv()
    for r in range(2):
        go(weights_copy(1, r, 0))
    to_sib(1, w_all.at[across])
    add(across)
    pending = [(1, w_all.at[other(across)], other(across))]
    for s in range(4):
        for stream in range(2):
            fresh_ones = []
            for r in range(2):
                weights_arrived(stream, r, s)
                if s < 3:
                    go(weights_copy(stream, r, s + 1))
                n = 2 + stream * 8 + s * 2 + r
                index = block_of(stream, r, s)
                to_sib(n, view(index, r, s))
                fresh_ones.append((n, index, r))
            for n, ref, index in pending:
                sib_arrived(n, ref)
                if index is not None:
                    add(index)
            pending = []
            for n, index, r in fresh_ones:
                whole = s < 3 or r == 1
                if whole:
                    add(index)
                pending.append((n, view(other(index), r, s), other(index) if whole else None))
        if s == 1:
            for n in range(3):
                arrived[m, n] = fresh[m, n]
            for o in range(1, NM):
                come = (m + NM - o) % NM
                remote(
                    fresh.at[m], arrived.at[come], st_send.at[o], st_recv.at[o], xn
                ).wait_recv()
            for h in range(NM):
                nm_ref[:, h, :] = arrived[h, 0]
                nf_ref[:, h, :] = arrived[h, 1]
                ns_ref[:, h, :] = arrived[h, 2]
    for n, ref, index in pending:
        sib_arrived(n, ref)
        if index is not None:
            add(index)
    kv_ref[...] = acc[...].astype(BF16)

    for copy in sends:
        copy.wait_send()

    @pl.when(jnp.logical_not(own_final))
    def _():
        final_copy(0).wait_send()


def on_device(acts, cotangent, master, first_moment, second_moment, long_acts):
    flat = [a.reshape(a.shape[0], -1) for a in (cotangent, master, first_moment, second_moment)]
    state_out = jax.ShapeDtypeStruct((ROWS // NM, NM, COL), F32)
    dma = pltpu.SemaphoreType.DMA
    outs = pl.pallas_call(
        kernel,
        out_shape=[state_out] * 3 + [jax.ShapeDtypeStruct((ROWS, COL), BF16)],
        in_specs=[pl.BlockSpec(memory_space=pl.ANY)] * 6,
        out_specs=[pl.BlockSpec(memory_space=pltpu.VMEM)] * 4,
        scratch_shapes=[
            pltpu.VMEM((TOK, FEAT), BF16),
            pltpu.VMEM((FEAT, TOK), BF16),
            pltpu.VMEM((NM, TOK, COL), BF16),
            pltpu.VMEM((NM, HALF, COL), F32),
            pltpu.VMEM((NM, HALF, COL), BF16),
            pltpu.VMEM((NM, HALF, COL), BF16),
            pltpu.VMEM((2, 2, NZ - 1, 2, CH, COL), BF16),
            pltpu.VMEM((2, 2, NZ - 1, 2, CH, COL), BF16),
            pltpu.VMEM((NM, CH, COL), BF16),
            pltpu.VMEM((2, 4, CH, COL), BF16),
            pltpu.VMEM((3, ROWS, COL), F32),
            pltpu.VMEM((NM, 3, ROWS // NM, COL), F32),
            pltpu.VMEM((NM, 3, ROWS // NM, COL), F32),
            pltpu.VMEM((ND, ROWS, COL), BF16),
            pltpu.VMEM((ROWS, ND * ROWS), BF16),
            pltpu.VMEM((ROWS, COL), F32),
            dma((6,)),
            dma((9,)),
            dma((9,)),
            dma((NM,)),
            dma((NM,)),
            dma((2, 2, NZ - 1)),
            dma((2, 2, NZ - 1)),
            dma((NM,)),
            dma((2, 4)),
            dma((NM,)),
            dma((NM,)),
            dma((2,)),
            dma((2, 2, 4)),
            dma((2, 2, 4)),
            dma((18,)),
            dma((18,)),
        ],
        compiler_params=pltpu.CompilerParams(
            collective_id=0, has_side_effects=True, vmem_limit_bytes=56 * 1024 * 1024
        ),
        cost_estimate=pl.CostEstimate(
            flops=2 * TOK * FEAT * NM * COL + 2 * ROWS * ND * ROWS * COL,
            bytes_accessed=8 * 1024 * 1024,
            transcendentals=0,
        ),
    )(acts, flat[0], flat[1], flat[2], flat[3], long_acts)
    return outs[0], outs[1], outs[2], outs[3].reshape(ROWS, 1, COL)


def solution(mesh):
    in_specs = (
        P("dp", "mp"),
        P("dp", "mp", None),
        P("dp", "mp", None),
        P("dp", "mp", None),
        P("dp", "mp", None),
        P("dp", None),
    )
    out_specs = (
        P(("dp", "mp"), None, None),
        P(("dp", "mp"), None, None),
        P(("dp", "mp"), None, None),
        P("dp", "mp", None),
    )
    return jax.shard_map(
        on_device, mesh=mesh, in_specs=in_specs, out_specs=out_specs, check_vma=False
    )
```

time: 657 us -> 135 us (0.21)
  waiting for transfers between devices: 585 us -> 0 us
  Pallas kernels: 0 us -> 124 us
  matrix products: 17.4 us -> 0 us
  between operations: 13.8 us -> 0.64 us
  blocking collectives: 10.3 us -> 0 us
  local copies, waits for them, and re-layouts: 18.2 us -> 10.1 us
  starting transfers between devices: 7.59 us -> 0 us
    all_gather x2 -> x0, waiting for transfers between devices: 416 us -> none  [the longest x1 334 us: on_device(): gathered = lax.all_gather(acts, 'mp', axis=1, tiled=True)]
    reduce_scatter x2 -> x0, waiting for transfers between devices: 154 us -> none  [the longest x1 124 us: on_device(): lax.psum_scatter(product.reshape(lax.axis_size('dp') * master.shape[0], m...]
    pallas_call x0 -> x1, Pallas kernels: none -> 124 us  [on_device(): pl.pallas_call(kernel, out_shape=[state_out] * 3 + [jax.ShapeDtypeStruct(...]
    dot_general x2 -> x0, matrix products: 17.4 us -> none  [the longest x1 12.5 us: on_device(): lax.dot_general(columns, flat_cot, (((0,), (0,)), ((), ())), preferred_el...]
    all_to_all x2 -> x0, waiting for transfers between devices: 14.2 us -> none  [the longest x1 8.65 us: on_device(): lax.all_to_all(second_next, 'mp', split_axis=0, concat_axis=1, tiled=True)]
    all_to_all x1 -> x0, blocking collectives: 10.3 us -> none  [on_device(): lax.all_to_all(master_next, 'mp', split_axis=0, concat_axis=1, tiled=True)]
    all_to_all x2 -> x0, starting transfers between devices: 7.43 us -> none  [the longest x1 4.02 us: on_device(): lax.all_to_all(first_next, 'mp', split_axis=0, concat_axis=1, tiled=True)]
    reshape x1 -> x0, local copies, waits for them, and re-layouts: 6.72 us -> none  [on_device(): piece.reshape(piece.shape[0], -1)]
  transfers between devices with their start and end apart: 6 -> 0, of which waited for: 6 -> 0; matrix products, arithmetic and copies ran while one was open for 2% -> 0% of each run, Pallas kernels for 0% -> 0%
where the time goes in v1:
time: 135 us
  Pallas kernels  124 us (92%)
  local copies, waits for them, and re-layouts  10.1 us (7%)
    pallas_call x1, Pallas kernels, on_device(): pl.pallas_call(kernel, out_shape=[state_out] * 3 + [jax.ShapeDtypeStruct(...  124 us
    unnamed x6, local copies, waits for them, and re-layouts  10.1 us

profile of v1, /device:TPU:1, one launch (start us, length us, event | category | flops | bytes accessed | tf_op | source)
XLA Modules:
  0.0 134.6 jit_solution(3550032197852799899)
XLA Ops:
  0.6 1.7 %copy.16 = f32[256,1,256]{2,0,1:T(8,128)} copy(f32[256,1,256]{2,1,0:T(1,128)} %param.8) | data formatting | bytes 524288
  2.3 1.9 %copy_bitcast_fusion = (f32[256,256]{1,0:T(8,128)}, f32[256,256]{1,0:T(8,128)}) fusion(f32[256,1,256]{2,1,0:T(1,128)} %param.10, f32[256,1,256]{2,1,0:T(1,128)} %param.9), kind=kLoop, calls=%fused_computation | loop fusion | bytes 1048576
  4.2 123.9 %shard_map.93 = (f32[32,8,256]{2,1,0:T(8,128)}, f32[32,8,256]{2,1,0:T(8,128)}, f32[32,8,256]{2,1,0:T(8,128)}, bf16[256,256]{1,0:T(8,128)(2,1)}) custom-call(bf16[1024,1024]{1,0:T(8,128)(2,1)} %acts_hbm.1, bf16[1024,256]{1,0:T(8,128)(2,1)} %bitcast.11, f32[256,256]{1,0:T(8,128)} %bitcast.9, f32[256,256]{1,0:T(8,128)} %get-tuple-element.13.fir_hbm, ...), custom_call_target="tpu_custom_call" | custom-call | flops 5368709120 | bytes 8388608 | tf_op jit(solution)/shard_map/pallas_call | solution.py:377
  128.0 1.7 %copy.21 = f32[32,8,256]{2,1,0:T(8,128)} copy(f32[32,8,256]{2,1,0:T(8,128)} %get-tuple-element.18) | data formatting | bytes 524288
  129.7 1.7 %copy.22 = f32[32,8,256]{2,1,0:T(8,128)} copy(f32[32,8,256]{2,1,0:T(8,128)} %get-tuple-element.19) | data formatting | bytes 524288
  131.4 1.7 %copy.23 = f32[32,8,256]{2,1,0:T(8,128)} copy(f32[32,8,256]{2,1,0:T(8,128)} %get-tuple-element.20) | data formatting | bytes 524288
  133.0 1.6 %copy.24 = bf16[256,1,256]{2,0,1:T(8,128)(2,1)} copy(bf16[256,1,256]{2,0,1:T(8,128)(2,1)} %bitcast.10) | data formatting | bytes 262144

commit v2 on v1

v2 whole, which is shorter than its diff:
```python
import jax
import jax.numpy as jnp
from jax import lax
from jax.experimental import pallas as pl
from jax.experimental.pallas import tpu as pltpu
from jax.sharding import PartitionSpec as P

beta_one = 0.9
beta_two = 0.95
learn_rate = 0.001
decay_rate = 0.1
adam_eps = 1e-08
steps_done = 100
fix_one = 1.0 - beta_one**steps_done
fix_two = 1.0 - beta_two**steps_done

F32, BF16 = jnp.float32, jnp.bfloat16
NZ = 8
NM = 8
ND = 32
FEAT = 1024
TOK = 1024
COL = 256
HALF = FEAT // 2
CH = HALF // NZ
ROWS = 256


def dp_index(xh, z, k):
    return xh * 16 + z * 2 + k


def mp_index(y, xl):
    return y * 2 + xl


def remote(src, dst, send_sem, recv_sem, dev):
    return pltpu.make_async_remote_copy(
        src_ref=src,
        dst_ref=dst,
        send_sem=send_sem,
        recv_sem=recv_sem,
        device_id=dev,
        device_id_type=pl.DeviceIdType.MESH,
    )


def adamw(master, first, second, grad):
    first_next = beta_one * first + (1.0 - beta_one) * grad
    second_next = beta_two * second + (1.0 - beta_two) * grad * grad
    update = (
        first_next / fix_one / (jnp.sqrt(second_next / fix_two) + adam_eps) + decay_rate * master
    )
    return master - learn_rate * update, first_next, second_next


def kernel(
    acts_hbm, cot_hbm, mas_hbm, fir_hbm, sec_hbm, long_hbm,
    nm_hbm, nf_hbm, ns_hbm, kv_hbm,
    acts_v, acts_t, cots, prod, pair_out, pair_in, ring_out, ring_in, fin, land,
    raw, state, lent, grad_out, grad_in, fresh, arrived, out_v, w_all, long_v, acc, kv_v,
    load_sem, out_sem, cot_send, cot_recv, pair_send, pair_recv, ring_send, ring_recv,
    fin_send, land_recv, pre_send, pre_recv, post_send, post_recv,
    st_send, st_recv, x_sem, wr_send, wr_recv, sib_send, sib_recv,
):
    d, m = lax.axis_index("dp"), lax.axis_index("mp")
    xh, z, k = d // 16, (d // 2) % NZ, d % 2
    y, xl = m // 2, m % 2
    up, down = (z + 1) % NZ, (z + NZ - 1) % NZ
    yp, ym, yo = (y + 1) % 4, (y + 3) % 4, (y + 2) % 4
    xn = (d, mp_index(y, 1 - xl))
    dev_yp, dev_ym = (d, mp_index(yp, xl)), (d, mp_index(ym, xl))
    sib = (dp_index(xh, z, 1 - k), m)
    dev_up, dev_down = (dp_index(xh, up, k), m), (dp_index(xh, down, k), m)
    xpart = (dp_index(1 - xh, z, k), m)
    dt = dp_index(m // 4, z, k)

    def lender(zi, ki):
        return 4 * (z % 2) + 2 * k + zi, ki

    def owner(q):
        return 2 * q + z // 4, (z // 2) % 2

    loads = [
        pltpu.make_async_copy(cot_hbm, cots.at[m], load_sem.at[0]),
        pltpu.make_async_copy(acts_hbm, acts_v, load_sem.at[1]),
        pltpu.make_async_copy(mas_hbm, raw.at[0], load_sem.at[2]),
        pltpu.make_async_copy(fir_hbm, raw.at[1], load_sem.at[3]),
        pltpu.make_async_copy(sec_hbm, raw.at[2], load_sem.at[4]),
        pltpu.make_async_copy(long_hbm, long_v, load_sem.at[5]),
    ]
    for load in loads[:5]:
        load.start()

    barrier = pltpu.get_barrier_semaphore()

    def greet(dev):
        pl.semaphore_signal(barrier, inc=1, device_id=dev, device_id_type=pl.DeviceIdType.MESH)

    for dev in (sib, dev_up, dev_down, xpart):
        greet(dev)
    for o in range(1, NM):
        greet((d, (m + o) % NM))
    for o in range(NM):
        greet((dt, (m + o) % NM))
    for a in range(2):
        for q in range(4):
            greet((dp_index(a, z, k), 4 * xh + q))
    for zi in range(2):
        for ki in range(2):
            zt, kt = lender(zi, ki)
            greet((dp_index(xh, zt, kt), m))
    for q in range(4):
        zo, ko = owner(q)
        greet((dp_index(xh, zo, ko), m))
    pl.semaphore_wait(barrier, 4 + NM - 1 + NM + 8 + 4 + 4)

    sends = []

    def go(copy):
        copy.start()
        sends.append(copy)
        return copy

    def go_or_keep(here, src, dst, send_sem, recv_sem, dev):
        @pl.when(here)
        def _():
            pltpu.make_async_copy(src, dst, recv_sem).start()

        @pl.when(jnp.logical_not(here))
        def _():
            remote(src, dst, send_sem, recv_sem, dev).start()

    def sent_or_kept(here, src, dst, send_sem, recv_sem, dev):
        @pl.when(jnp.logical_not(here))
        def _():
            remote(src, dst, send_sem, recv_sem, dev).wait_send()

    head = [
        m, mp_index(y, 1 - xl), mp_index(ym, xl), mp_index(yp, xl),
        mp_index(yo, xl), mp_index(ym, 1 - xl), mp_index(yp, 1 - xl), mp_index(yo, 1 - xl),
    ]
    low, high = pl.ds(0, TOK // 2), pl.ds(TOK // 2, TOK // 2)

    def cot_copy(n, block, dev):
        return remote(block, block, cot_send.at[n], cot_recv.at[n], dev)

    def cot_arrived(n, block):
        cot_copy(n, block, xn).wait_recv()

    def product(j):
        def tile(i, carry):
            rows = pl.multiple_of((1 - k) * HALF + i * 256, 256)
            pair_out[j, pl.ds(pl.multiple_of(i * 256, 256), 256), :] = jnp.dot(
                acts_t[pl.ds(rows, 256), :], cots[head[j]], preferred_element_type=F32
            ).astype(BF16)
            return carry

        lax.fori_loop(0, HALF // 256, tile, 0)
        go(remote(pair_out.at[j], pair_in.at[j], pair_send.at[j], pair_recv.at[j], sib))

        def mine(i, carry):
            rows = pl.multiple_of(k * HALF + i * 256, 256)
            prod[j, pl.ds(pl.multiple_of(i * 256, 256), 256), :] = jnp.dot(
                acts_t[pl.ds(rows, 256), :], cots[head[j]], preferred_element_type=F32
            )
            return carry

        lax.fori_loop(0, HALF // 256, mine, 0)

    def pair_arrived(j):
        remote(pair_out.at[j], pair_in.at[j], pair_send.at[j], pair_recv.at[j], sib).wait_recv()

    def ring_copy(g, r, s):
        return remote(
            ring_out.at[g, r, s], ring_in.at[g, r, s], ring_send.at[g, r, s], ring_recv.at[g, r, s],
            (dev_up, dev_down)[r],
        )

    def ring(g, s):
        for r in range(2):
            j = 2 * g + r
            chunk = (z + 2 * NZ - 1 - s) % NZ if r == 0 else (z + 1 + s) % NZ
            rows = pl.ds(pl.multiple_of(chunk * CH, CH), CH)
            total = prod[j, rows, :] + pair_in[j, rows, :].astype(F32)
            if s > 0:
                ring_copy(g, r, s - 1).wait_recv()
                total = total + ring_in[g, r, s - 1].astype(F32)
            if s < NZ - 1:
                ring_out[g, r, s] = total.astype(BF16)
                go(ring_copy(g, r, s))
            else:
                fin[j] = total.astype(BF16)
                hand_over(j)

    def final_args(j):
        slot = (xh, m % 4)
        return (
            dt == d, fin.at[j], land.at[slot], fin_send.at[j], land_recv.at[slot], (dt, head[j])
        )

    def hand_over(j):
        if j > 0:
            go(remote(*final_args(j)[1:]))
        else:
            go_or_keep(*final_args(0))

    loads[0].wait()
    own = cots.at[m]
    go(cot_copy(0, own, xn))
    go(cot_copy(1, own, dev_yp))
    go(cot_copy(2, own, dev_ym))

    def lend_args(zi, ki):
        zt, kt = lender(zi, ki)
        rows = pl.ds(zi * 2 * CH + ki * CH, CH)
        return (
            (zt == z) & (kt == k), state.at[:, rows, :], lent.at[z // 2],
            pre_send.at[2 * zi + ki], pre_recv.at[z // 2], (dp_index(xh, zt, kt), m),
        )

    for n in range(3):
        loads[2 + n].wait()
        state[n] = raw[n, :, 0, :]
    for zi in range(2):
        for ki in range(2):
            go_or_keep(*lend_args(zi, ki))
    loads[5].start()
    loads[1].wait()

    def turn(i, carry):
        block = acts_v[:, pl.ds(pl.multiple_of(i * 2 * CH, 2 * CH), 2 * CH)].T
        at = pl.multiple_of(i * CH, CH)
        acts_t[pl.ds(at, CH), :] = block[:CH]
        acts_t[pl.ds(at + HALF, CH), :] = block[CH:]
        return carry

    lax.fori_loop(0, NZ, turn, 0)
    product(0)
    cot_arrived(1, cots.at[head[2]])
    go(cot_copy(3, cots.at[head[2], low], dev_yp))
    cot_arrived(2, cots.at[head[3]])
    go(cot_copy(4, cots.at[head[3], high], dev_ym))
    cot_arrived(0, cots.at[head[1]])
    go(cot_copy(5, cots.at[head[1]], dev_yp))
    go(cot_copy(6, cots.at[head[1]], dev_ym))
    product(1)
    product(2)
    product(3)
    for j in range(2):
        pair_arrived(j)
    ring(0, 0)
    for j in range(2, 4):
        pair_arrived(j)
    ring(1, 0)
    cot_arrived(3, cots.at[head[4], low])
    go(cot_copy(7, cots.at[head[4], low], xn))
    cot_arrived(4, cots.at[head[4], high])
    go(cot_copy(8, cots.at[head[4], high], xn))
    product(4)
    for s in range(1, NZ - 1):
        ring(0, s)
        ring(1, s)
    cot_arrived(5, cots.at[head[5]])
    product(5)
    cot_arrived(6, cots.at[head[6]])
    product(6)
    pair_arrived(4)
    pair_arrived(5)
    ring(2, 0)
    cot_arrived(7, cots.at[head[7], low])
    cot_arrived(8, cots.at[head[7], high])
    product(7)
    pair_arrived(6)
    pair_arrived(7)
    ring(3, 0)
    ring(0, NZ - 1)
    ring(1, NZ - 1)
    for s in range(1, NZ):
        ring(2, s)
        ring(3, s)

    place = xh * NZ + z
    half_rows = pl.ds(pl.multiple_of(k * CH, CH), CH)
    for q in range(4):
        remote(
            state.at[:, pl.ds(0, CH), :], lent.at[q], pre_send.at[0], pre_recv.at[q], xn
        ).wait_recv()
    for q in range(4):
        for a in range(2):
            remote(
                fin.at[0], land.at[a, q], fin_send.at[0], land_recv.at[a, q], xn
            ).wait_recv()
        grad = (land[0, q].astype(F32) + land[1, q].astype(F32)).astype(BF16)
        grad_out[q] = grad
        w_all[place, q, half_rows, :] = adamw(
            lent[q, 0], lent[q, 1], lent[q, 2], grad.astype(F32)
        )[0].astype(BF16)

    other_rows = pl.ds(pl.multiple_of((1 - k) * CH, CH), CH)

    def view(at, r=0, s=0, rows=half_rows):
        if s < 3:
            return w_all.at[at, :, rows, :]
        return w_all.at[at, pl.ds(2 * r, 2), rows, :]

    w_own = view(place)
    go(remote(w_own, w_own, x_sem.at[0], x_sem.at[1], xpart))

    def block_of(stream, r, s):
        at = (z + NZ - 1 - s) % NZ if r == 0 else (z + 1 + s) % NZ
        return (xh if stream == 0 else 1 - xh) * NZ + at

    def weights_copy(stream, r, s):
        src = view(block_of(stream, r, s - 1), r, s)
        return remote(
            src, src, wr_send.at[stream, r, s], wr_recv.at[stream, r, s], (dev_up, dev_down)[r]
        )

    def weights_arrived(stream, r, s):
        dst = view(block_of(stream, r, s), r, s)
        remote(
            dst, dst, wr_send.at[stream, r, s], wr_recv.at[stream, r, s], (dev_up, dev_down)[r]
        ).wait_recv()

    def to_sib(n, ref):
        go(remote(ref, ref, sib_send.at[n], sib_recv.at[n], sib))

    def sib_arrived(n, ref):
        remote(ref, ref, sib_send.at[n], sib_recv.at[n], sib).wait_recv()

    for r in range(2):
        go(weights_copy(0, r, 0))
    to_sib(0, w_own)

    def post_args(q):
        zo, ko = owner(q)
        slot = 2 * (z % 2) + k
        return (
            (zo == z) & (ko == k), grad_out.at[q], grad_in.at[slot],
            post_send.at[q], post_recv.at[slot], (dp_index(xh, zo, ko), m),
        )

    for q in range(4):
        go_or_keep(*post_args(q))

    loads[5].wait()

    def add(at, start=False):
        value = 0.0
        for q in range(4):
            cols = ((at // NZ) * 4 + q) * FEAT + (at % NZ) * 2 * CH
            value += jnp.dot(
                long_v[:, pl.ds(pl.multiple_of(cols, 2 * CH), 2 * CH)],
                w_all[at, q],
                preferred_element_type=F32,
            )
        if start:
            acc[...] = value
        else:
            acc[...] += value

    across = (1 - xh) * NZ + z
    w_across = view(across)
    remote(w_across, w_across, x_sem.at[0], x_sem.at[1], xpart).wait_recv()
    for r in range(2):
        go(weights_copy(1, r, 0))
    to_sib(1, w_across)
    sib_arrived(0, view(place, rows=other_rows))
    add(place, True)

    def state_copy(o):
        to = (m + o) % NM
        return remote(fresh.at[to], arrived.at[m], st_send.at[o], st_recv.at[o], (d, to))

    outs = [
        pltpu.make_async_copy(out_v.at[n], ref, out_sem.at[n])
        for n, ref in enumerate((nm_hbm, nf_hbm, ns_hbm))
    ]
    pending = [(1, view(across, rows=other_rows), across)]
    for s in range(4):
        for stream in range(2):
            come = []
            for r in range(2):
                weights_arrived(stream, r, s)
                if s < 3:
                    go(weights_copy(stream, r, s + 1))
                n = 2 + stream * 8 + s * 2 + r
                at = block_of(stream, r, s)
                to_sib(n, view(at, r, s))
                whole = s < 3 or r == 1
                come.append((n, view(at, r, s, other_rows), at if whole else None))
            for n, ref, at in pending:
                sib_arrived(n, ref)
                if at is not None:
                    add(at)
            pending = come
        if s == 0:
            for n in range(4):
                remote(
                    grad_out.at[0], grad_in.at[n], post_send.at[0], post_recv.at[n], xn
                ).wait_recv()
                rows = pl.ds(n * CH, CH)
                new = adamw(
                    state[0, rows, :], state[1, rows, :], state[2, rows, :], grad_in[n].astype(F32)
                )
                for a, value in enumerate(new):
                    fresh[2 * n, a] = value[: CH // 2]
                    fresh[2 * n + 1, a] = value[CH // 2 :]
            for o in range(1, NM):
                go(state_copy(o))
        if s == 2:
            for a in range(3):
                arrived[m, a] = fresh[m, a]
            for o in range(1, NM):
                at = (m + NM - o) % NM
                remote(fresh.at[m], arrived.at[at], st_send.at[o], st_recv.at[o], xn).wait_recv()
            for a in range(3):
                for h in range(NM):
                    out_v[a, :, h, :] = arrived[h, a]
                outs[a].start()
    for n, ref, at in pending:
        sib_arrived(n, ref)
        if at is not None:
            add(at)
    kv_v[...] = acc[...].astype(BF16)
    kv_out = pltpu.make_async_copy(kv_v, kv_hbm, out_sem.at[3])
    kv_out.start()

    for copy in sends:
        copy.wait_send()
    sent_or_kept(*final_args(0))
    for n in range(4):
        sent_or_kept(*lend_args(n // 2, n % 2))
        sent_or_kept(*post_args(n))
    for out in outs:
        out.wait()
    kv_out.wait()


def settle(a_hbm, b_hbm, c_hbm, e_hbm, ao_hbm, bo_hbm, co_hbm, eo_hbm, sem):
    pairs = ((a_hbm, ao_hbm), (b_hbm, bo_hbm), (c_hbm, co_hbm), (e_hbm, eo_hbm))
    copies = [pltpu.make_async_copy(a, b, sem.at[n]) for n, (a, b) in enumerate(pairs)]
    for copy in copies:
        copy.start()
    for copy in copies:
        copy.wait()


def on_device(acts, cotangent, master, first_moment, second_moment, long_acts):
    state_out = jax.ShapeDtypeStruct((ROWS // NM, NM, COL), F32)
    out_shape = [state_out] * 3 + [jax.ShapeDtypeStruct((ROWS, COL), BF16)]
    dma = pltpu.SemaphoreType.DMA
    anywhere = pl.BlockSpec(memory_space=pl.ANY)
    outs = pl.pallas_call(
        kernel,
        out_shape=out_shape,
        in_specs=[anywhere] * 6,
        out_specs=[anywhere] * 4,
        scratch_shapes=[
            pltpu.VMEM((TOK, FEAT), BF16),
            pltpu.VMEM((FEAT, TOK), BF16),
            pltpu.VMEM((NM, TOK, COL), BF16),
            pltpu.VMEM((NM, HALF, COL), F32),
            pltpu.VMEM((NM, HALF, COL), BF16),
            pltpu.VMEM((NM, HALF, COL), BF16),
            pltpu.VMEM((4, 2, NZ - 1, CH, COL), BF16),
            pltpu.VMEM((4, 2, NZ - 1, CH, COL), BF16),
            pltpu.VMEM((NM, CH, COL), BF16),
            pltpu.VMEM((2, 4, CH, COL), BF16),
            pltpu.VMEM((3, ROWS, 1, COL), F32),
            pltpu.VMEM((3, ROWS, COL), F32),
            pltpu.VMEM((4, 3, CH, COL), F32),
            pltpu.VMEM((4, CH, COL), BF16),
            pltpu.VMEM((4, CH, COL), BF16),
            pltpu.VMEM((NM, 3, ROWS // NM, COL), F32),
            pltpu.VMEM((NM, 3, ROWS // NM, COL), F32),
            pltpu.VMEM((3, ROWS // NM, NM, COL), F32),
            pltpu.VMEM((ND // 2, 4, 2 * CH, COL), BF16),
            pltpu.VMEM((ROWS, ND * ROWS), BF16),
            pltpu.VMEM((ROWS, COL), F32),
            pltpu.VMEM((ROWS, COL), BF16),
            dma((6,)),
            dma((4,)),
            dma((9,)),
            dma((9,)),
            dma((NM,)),
            dma((NM,)),
            dma((4, 2, NZ - 1)),
            dma((4, 2, NZ - 1)),
            dma((NM,)),
            dma((2, 4)),
            dma((4,)),
            dma((4,)),
            dma((4,)),
            dma((4,)),
            dma((NM,)),
            dma((NM,)),
            dma((2,)),
            dma((2, 2, 4)),
            dma((2, 2, 4)),
            dma((18,)),
            dma((18,)),
        ],
        compiler_params=pltpu.CompilerParams(
            collective_id=0, has_side_effects=True, vmem_limit_bytes=56 * 1024 * 1024
        ),
        cost_estimate=pl.CostEstimate(
            flops=2 * TOK * FEAT * NM * COL + 2 * ROWS * ND * ROWS * COL,
            bytes_accessed=8 * 1024 * 1024,
            transcendentals=0,
        ),
    )(acts, cotangent.reshape(TOK, COL), master, first_moment, second_moment, long_acts)
    outs = pl.pallas_call(
        settle,
        out_shape=out_shape,
        in_specs=[anywhere] * 4,
        out_specs=[anywhere] * 4,
        scratch_shapes=[dma((4,))],
    )(*outs)
    return outs[0], outs[1], outs[2], outs[3].reshape(ROWS, 1, COL)


def solution(mesh):
    in_specs = (
        P("dp", "mp"),
        P("dp", "mp", None),
        P("dp", "mp", None),
        P("dp", "mp", None),
        P("dp", "mp", None),
        P("dp", None),
    )
    out_specs = (
        P(("dp", "mp"), None, None),
        P(("dp", "mp"), None, None),
        P(("dp", "mp"), None, None),
        P("dp", "mp", None),
    )
    return jax.shard_map(
        on_device, mesh=mesh, in_specs=in_specs, out_specs=out_specs, check_vma=False
    )
```

time: 135 us -> 143 us (1.059)
  Pallas kernels: 124 us -> 142 us
  local copies, waits for them, and re-layouts: 10.1 us -> 0 us
    pallas_call x1 -> x2, Pallas kernels: 124 us -> 142 us  [the longest x1 113 us: on_device(): pl.pallas_call(kernel, out_shape=out_shape, in_specs=[anywhere] * 6, out_...]
    unnamed x6 -> x0, local copies, waits for them, and re-layouts: 10.1 us -> none
where the time goes in v2:
time: 143 us
  Pallas kernels  142 us (99%)
    pallas_call x1, Pallas kernels, on_device(): pl.pallas_call(kernel, out_shape=out_shape, in_specs=[anywhere] * 6, out_...  113 us
    pallas_call x1, Pallas kernels, on_device(): pl.pallas_call(settle, out_shape=out_shape, in_specs=[anywhere] * 4, out_...  28.9 us

profile of v2, /device:TPU:1, one launch (start us, length us, event | category | flops | bytes accessed | tf_op | source)
XLA Modules:
  0.0 142.6 jit_solution(1267279015465022725)
XLA Ops:
  0.6 113.0 %shard_map.93 = (f32[32,8,256]{2,1,0:T(8,128)}, f32[32,8,256]{2,1,0:T(8,128)}, f32[32,8,256]{2,1,0:T(8,128)}, bf16[256,256]{1,0:T(8,128)(2,1)}) custom-call(bf16[1024,1024]{1,0:T(8,128)(2,1)} %acts_hbm.1, bf16[1024,256]{1,0:T(8,128)(2,1)} %bitcast.2, f32[256,1,256]{2,1,0:T(1,128)} %mas_hbm.1, f32[256,1,256]{2,1,0:T(1,128)} %fir_hbm.1, ...), custom_call_target="tpu_custom_call" | custom-call | flops 5368709120 | bytes 8388608 | tf_op jit(solution)/shard_map/pallas_call | solution.py:455
  113.6 28.9 %shard_map.94 = (f32[32,8,256]{2,1,0:T(8,128)}, f32[32,8,256]{2,1,0:T(8,128)}, f32[32,8,256]{2,1,0:T(8,128)}, bf16[256,256]{1,0:T(8,128)(2,1)}) custom-call(f32[32,8,256]{2,1,0:T(8,128)} %get-tuple-element.12.a_hbm, f32[32,8,256]{2,1,0:T(8,128)} %get-tuple-element.13.b_hbm, f32[32,8,256]{2,1,0:T(8,128)} %get-tuple-element.14.c_hbm, ...), custom_call_target="tpu_custom_call" | custom-call | tf_op jit(solution)/shard_map/pallas_call | solution.py:514

commit v3 on v2

--- a/solution.py
+++ b/solution.py
@@ -61,7 +61,7 @@
     raw, state, lent, grad_out, grad_in, fresh, arrived, out_v, w_all, long_v, acc, kv_v,
     load_sem, out_sem, cot_send, cot_recv, pair_send, pair_recv, ring_send, ring_recv,
     fin_send, land_recv, pre_send, pre_recv, post_send, post_recv,
-    st_send, st_recv, x_sem, wr_send, wr_recv, sib_send, sib_recv,
+    st_send, st_recv, x_send, x_recv, wr_send, wr_recv, sib_send, sib_recv,
 ):
     d, m = lax.axis_index("dp"), lax.axis_index("mp")
     xh, z, k = d // 16, (d // 2) % NZ, d % 2
@@ -171,27 +171,47 @@
     def pair_arrived(j):
         remote(pair_out.at[j], pair_in.at[j], pair_send.at[j], pair_recv.at[j], sib).wait_recv()
 
-    def ring_copy(g, r, s):
+    def part(s, r):
+        return pl.ds(r * CH // 2, CH // 2) if s == 0 else pl.ds(0, CH)
+
+    def ring_copy(j, r, s):
         return remote(
-            ring_out.at[g, r, s], ring_in.at[g, r, s], ring_send.at[g, r, s], ring_recv.at[g, r, s],
-            (dev_up, dev_down)[r],
+            ring_out.at[j, r, s, part(s, r)], ring_in.at[j, r, s, part(s, r)],
+            ring_send.at[j, r, s], ring_recv.at[j, r, s], (dev_up, dev_down)[r],
         )
 
-    def ring(g, s):
+    def own_part(j, chunk, first, size):
+        rows = pl.ds(pl.multiple_of(chunk * CH + first, CH // 2), size)
+        return prod[j, rows, :] + pair_in[j, rows, :].astype(F32)
+
+    def ring(j, s):
         for r in range(2):
-            j = 2 * g + r
-            chunk = (z + 2 * NZ - 1 - s) % NZ if r == 0 else (z + 1 + s) % NZ
-            rows = pl.ds(pl.multiple_of(chunk * CH, CH), CH)
-            total = prod[j, rows, :] + pair_in[j, rows, :].astype(F32)
-            if s > 0:
-                ring_copy(g, r, s - 1).wait_recv()
-                total = total + ring_in[g, r, s - 1].astype(F32)
-            if s < NZ - 1:
-                ring_out[g, r, s] = total.astype(BF16)
-                go(ring_copy(g, r, s))
+            chunk = (z + NZ // 2 - s) % NZ if r == 0 else (z + NZ // 2 + s) % NZ
+            if s == 0:
+                ring_out[j, r, s, part(s, r)] = own_part(
+                    j, chunk, r * CH // 2, CH // 2
+                ).astype(BF16)
+            elif s == 1:
+                mine, theirs = part(0, r), part(0, 1 - r)
+                ring_out[j, r, s, theirs] = own_part(
+                    j, chunk, (1 - r) * CH // 2, CH // 2
+                ).astype(BF16)
+                total = own_part(j, chunk, r * CH // 2, CH // 2)
+                ring_copy(j, r, 0).wait_recv()
+                ring_out[j, r, s, mine] = (total + ring_in[j, r, 0, mine].astype(F32)).astype(BF16)
             else:
-                fin[j] = total.astype(BF16)
-                hand_over(j)
+                total = own_part(j, chunk, 0, CH)
+                ring_copy(j, r, s - 1).wait_recv()
+                ring_out[j, r, s] = (total + ring_in[j, r, s - 1].astype(F32)).astype(BF16)
+            go(ring_copy(j, r, s))
+
+    def finish(j):
+        total = own_part(j, z, 0, CH)
+        for r in range(2):
+            ring_copy(j, r, 3).wait_recv()
+            total = total + ring_in[j, r, 3].astype(F32)
+        fin[j] = total.astype(BF16)
+        hand_over(j)
 
     def final_args(j):
         slot = (xh, m % 4)
@@ -206,10 +226,15 @@
             go_or_keep(*final_args(0))
 
     loads[0].wait()
-    own = cots.at[m]
-    go(cot_copy(0, own, xn))
-    go(cot_copy(1, own, dev_yp))
-    go(cot_copy(2, own, dev_ym))
+    def half(j, side):
+        return cots.at[head[j], (low, high)[side]]
+
+    go(cot_copy(0, half(0, 0), xn))
+    go(cot_copy(2, half(0, 0), dev_yp))
+    go(cot_copy(4, half(0, 1), dev_ym))
+    go(cot_copy(1, half(0, 1), xn))
+    go(cot_copy(3, half(0, 1), dev_yp))
+    go(cot_copy(5, half(0, 0), dev_ym))
 
     def lend_args(zi, ki):
         zt, kt = lender(zi, ki)
@@ -237,48 +262,53 @@
 
     lax.fori_loop(0, NZ, turn, 0)
     product(0)
-    cot_arrived(1, cots.at[head[2]])
-    go(cot_copy(3, cots.at[head[2], low], dev_yp))
-    cot_arrived(2, cots.at[head[3]])
-    go(cot_copy(4, cots.at[head[3], high], dev_ym))
-    cot_arrived(0, cots.at[head[1]])
-    go(cot_copy(5, cots.at[head[1]], dev_yp))
-    go(cot_copy(6, cots.at[head[1]], dev_ym))
+    cot_arrived(2, half(2, 0))
+    go(cot_copy(6, half(2, 0), dev_yp))
+    cot_arrived(4, half(3, 1))
+    go(cot_copy(7, half(3, 1), dev_ym))
+    for side in range(2):
+        cot_arrived(side, half(1, side))
+        go(cot_copy(8 + side, half(1, side), dev_yp))
+        go(cot_copy(10 + side, half(1, side), dev_ym))
     product(1)
+    cot_arrived(3, half(2, 1))
     product(2)
+    cot_arrived(5, half(3, 0))
     product(3)
-    for j in range(2):
+    for j in range(4):
         pair_arrived(j)
-    ring(0, 0)
-    for j in range(2, 4):
+        ring(j, 0)
+    cot_arrived(6, half(4, 0))
+    go(cot_copy(12, half(4, 0), xn))
+    cot_arrived(7, half(4, 1))
+    go(cot_copy(13, half(4, 1), xn))
+    product(4)
+    for j in range(4):
+        ring(j, 1)
+    pair_arrived(4)
+    ring(4, 0)
+    for s in range(2, 4):
+        for j in range(4):
+            ring(j, s)
+        ring(4, s - 1)
+    for j in range(5, 8):
+        for side in range(2):
+            cot_arrived(2 * j - 2 + side, half(j, side))
+        product(j)
+    for j in range(5, 8):
         pair_arrived(j)
-    ring(1, 0)
-    cot_arrived(3, cots.at[head[4], low])
-    go(cot_copy(7, cots.at[head[4], low], xn))
-    cot_arrived(4, cots.at[head[4], high])
-    go(cot_copy(8, cots.at[head[4], high], xn))
-    product(4)
-    for s in range(1, NZ - 1):
-        ring(0, s)
-        ring(1, s)
-    cot_arrived(5, cots.at[head[5]])
-    product(5)
-    cot_arrived(6, cots.at[head[6]])
-    product(6)
-    pair_arrived(4)
-    pair_arrived(5)
-    ring(2, 0)
-    cot_arrived(7, cots.at[head[7], low])
-    cot_arrived(8, cots.at[head[7], high])
-    product(7)
-    pair_arrived(6)
-    pair_arrived(7)
-    ring(3, 0)
-    ring(0, NZ - 1)
-    ring(1, NZ - 1)
-    for s in range(1, NZ):
-        ring(2, s)
-        ring(3, s)
+        ring(j, 0)
+    ring(4, 3)
+    for j in range(4):
+        finish(j)
+    for j in range(5, 8):
+        ring(j, 1)
+    finish(4)
+    for s in range(2, 4):
+        for j in range(5, 8):
+            ring(j, s)
+    for j in range(5, 8):
+        finish(j)
 
     place = xh * NZ + z
     half_rows = pl.ds(pl.multiple_of(k * CH, CH), CH)
@@ -299,28 +329,31 @@
 
     other_rows = pl.ds(pl.multiple_of((1 - k) * CH, CH), CH)
 
-    def view(at, r=0, s=0, rows=half_rows):
-        if s < 3:
-            return w_all.at[at, :, rows, :]
-        return w_all.at[at, pl.ds(2 * r, 2), rows, :]
-
-    w_own = view(place)
-    go(remote(w_own, w_own, x_sem.at[0], x_sem.at[1], xpart))
+    def view(at, p, rows=half_rows):
+        return w_all.at[at, pl.ds(2 * p, 2), rows, :]
+
+    def x_copy(at, p):
+        return remote(view(at, p), view(at, p), x_send.at[p], x_recv.at[p], xpart)
 
     def block_of(stream, r, s):
         at = (z + NZ - 1 - s) % NZ if r == 0 else (z + 1 + s) % NZ
         return (xh if stream == 0 else 1 - xh) * NZ + at
 
-    def weights_copy(stream, r, s):
-        src = view(block_of(stream, r, s - 1), r, s)
+    def halves(r, s):
+        return range(2) if s < 3 else (r,)
+
+    def weights_copy(stream, r, s, p):
+        src = view(block_of(stream, r, s - 1), p)
         return remote(
-            src, src, wr_send.at[stream, r, s], wr_recv.at[stream, r, s], (dev_up, dev_down)[r]
+            src, src, wr_send.at[stream, r, s, p], wr_recv.at[stream, r, s, p],
+            (dev_up, dev_down)[r],
         )
 
-    def weights_arrived(stream, r, s):
-        dst = view(block_of(stream, r, s), r, s)
+    def weights_arrived(stream, r, s, p):
+        dst = view(block_of(stream, r, s), p)
         remote(
-            dst, dst, wr_send.at[stream, r, s], wr_recv.at[stream, r, s], (dev_up, dev_down)[r]
+            dst, dst, wr_send.at[stream, r, s, p], wr_recv.at[stream, r, s, p],
+            (dev_up, dev_down)[r],
         ).wait_recv()
 
     def to_sib(n, ref):
@@ -329,9 +362,12 @@
     def sib_arrived(n, ref):
         remote(ref, ref, sib_send.at[n], sib_recv.at[n], sib).wait_recv()
 
-    for r in range(2):
-        go(weights_copy(0, r, 0))
-    to_sib(0, w_own)
+    for p in range(2):
+        go(x_copy(place, p))
+        for r in range(2):
+            go(weights_copy(0, r, 0, p))
+    for p in range(2):
+        to_sib(p, view(place, p))
 
     def post_args(q):
         zo, ko = owner(q)
@@ -361,12 +397,13 @@
             acc[...] += value
 
     across = (1 - xh) * NZ + z
-    w_across = view(across)
-    remote(w_across, w_across, x_sem.at[0], x_sem.at[1], xpart).wait_recv()
-    for r in range(2):
-        go(weights_copy(1, r, 0))
-    to_sib(1, w_across)
-    sib_arrived(0, view(place, rows=other_rows))
+    for p in range(2):
+        x_copy(across, p).wait_recv()
+        for r in range(2):
+            go(weights_copy(1, r, 0, p))
+        to_sib(2 + p, view(across, p))
+    for p in range(2):
+        sib_arrived(p, view(place, p, other_rows))
     add(place, True)
 
     def state_copy(o):
@@ -377,23 +414,27 @@
         pltpu.make_async_copy(out_v.at[n], ref, out_sem.at[n])
         for n, ref in enumerate((nm_hbm, nf_hbm, ns_hbm))
     ]
-    pending = [(1, view(across, rows=other_rows), across)]
+    pending = [(2, across, 0, False), (3, across, 1, True)]
+
+    def catch_up():
+        for n, at, p, last in pending:
+            sib_arrived(n, view(at, p, other_rows))
+            if last:
+                add(at)
+
     for s in range(4):
         for stream in range(2):
             come = []
             for r in range(2):
-                weights_arrived(stream, r, s)
-                if s < 3:
-                    go(weights_copy(stream, r, s + 1))
-                n = 2 + stream * 8 + s * 2 + r
-                at = block_of(stream, r, s)
-                to_sib(n, view(at, r, s))
-                whole = s < 3 or r == 1
-                come.append((n, view(at, r, s, other_rows), at if whole else None))
-            for n, ref, at in pending:
-                sib_arrived(n, ref)
-                if at is not None:
-                    add(at)
+                for p in halves(r, s):
+                    weights_arrived(stream, r, s, p)
+                    if s < 2 or (s == 2 and p == r):
+                        go(weights_copy(stream, r, s + 1, p))
+                    n = 4 + stream * 16 + s * 4 + r * 2 + p
+                    at = block_of(stream, r, s)
+                    to_sib(n, view(at, p))
+                    come.append((n, at, p, p == 1))
+            catch_up()
             pending = come
         if s == 0:
             for n in range(4):
@@ -419,10 +460,7 @@
                 for h in range(NM):
                     out_v[a, :, h, :] = arrived[h, a]
                 outs[a].start()
-    for n, ref, at in pending:
-        sib_arrived(n, ref)
-        if at is not None:
-            add(at)
+    catch_up()
     kv_v[...] = acc[...].astype(BF16)
     kv_out = pltpu.make_async_copy(kv_v, kv_hbm, out_sem.at[3])
     kv_out.start()
@@ -438,8 +476,8 @@
     kv_out.wait()
 
 
-def settle(a_hbm, b_hbm, c_hbm, e_hbm, ao_hbm, bo_hbm, co_hbm, eo_hbm, sem):
-    pairs = ((a_hbm, ao_hbm), (b_hbm, bo_hbm), (c_hbm, co_hbm), (e_hbm, eo_hbm))
+def settle(a_ref, b_ref, c_ref, e_ref, a_hbm, b_hbm, c_hbm, e_hbm, sem):
+    pairs = ((a_ref, a_hbm), (b_ref, b_hbm), (c_ref, c_hbm), (e_ref, e_hbm))
     copies = [pltpu.make_async_copy(a, b, sem.at[n]) for n, (a, b) in enumerate(pairs)]
     for copy in copies:
         copy.start()
@@ -464,8 +502,8 @@
             pltpu.VMEM((NM, HALF, COL), F32),
             pltpu.VMEM((NM, HALF, COL), BF16),
             pltpu.VMEM((NM, HALF, COL), BF16),
-            pltpu.VMEM((4, 2, NZ - 1, CH, COL), BF16),
-            pltpu.VMEM((4, 2, NZ - 1, CH, COL), BF16),
+            pltpu.VMEM((NM, 2, 4, CH, COL), BF16),
+            pltpu.VMEM((NM, 2, 4, CH, COL), BF16),
             pltpu.VMEM((NM, CH, COL), BF16),
             pltpu.VMEM((2, 4, CH, COL), BF16),
             pltpu.VMEM((3, ROWS, 1, COL), F32),
@@ -482,12 +520,12 @@
             pltpu.VMEM((ROWS, COL), BF16),
             dma((6,)),
             dma((4,)),
-            dma((9,)),
-            dma((9,)),
+            dma((14,)),
+            dma((14,)),
             dma((NM,)),
             dma((NM,)),
-            dma((4, 2, NZ - 1)),
-            dma((4, 2, NZ - 1)),
+            dma((NM, 2, 4)),
+            dma((NM, 2, 4)),
             dma((NM,)),
             dma((2, 4)),
             dma((4,)),
@@ -497,10 +535,11 @@
             dma((NM,)),
             dma((NM,)),
             dma((2,)),
-            dma((2, 2, 4)),
-            dma((2, 2, 4)),
-            dma((18,)),
-            dma((18,)),
+            dma((2,)),
+            dma((2, 2, 4, 2)),
+            dma((2, 2, 4, 2)),
+            dma((36,)),
+            dma((36,)),
         ],
         compiler_params=pltpu.CompilerParams(
             collective_id=0, has_side_effects=True, vmem_limit_bytes=56 * 1024 * 1024
@@ -514,7 +553,7 @@
     outs = pl.pallas_call(
         settle,
         out_shape=out_shape,
-        in_specs=[anywhere] * 4,
+        in_specs=[pl.BlockSpec(memory_space=pltpu.VMEM)] * 4,
         out_specs=[anywhere] * 4,
         scratch_shapes=[dma((4,))],
     )(*outs)

time: 143 us -> 99.3 us (0.69)
  Pallas kernels: 142 us -> 98.2 us
    pallas_call x1, Pallas kernels: 28.9 us -> 2.09 us  [on_device(): pl.pallas_call(settle, out_shape=out_shape, in_specs=[pl.BlockSpec(memory...]
    pallas_call x1, Pallas kernels: 113 us -> 96.1 us  [on_device(): pl.pallas_call(kernel, out_shape=out_shape, in_specs=[anywhere] * 6, out_...]
where the time goes in v3:
time: 99.3 us; the launch traced here: 98.9 us
  Pallas kernels  98.2 us (99%)
    pallas_call x1, Pallas kernels, on_device(): pl.pallas_call(kernel, out_shape=out_shape, in_specs=[anywhere] * 6, out_...  96.1 us
    pallas_call x1, Pallas kernels, on_device(): pl.pallas_call(settle, out_shape=out_shape, in_specs=[pl.BlockSpec(memory...  2.09 us

profile of v3, /device:TPU:1, one launch (start us, length us, event | category | flops | bytes accessed | tf_op | source)
XLA Modules:
  0.0 98.9 jit_solution(4230740142714396589)
XLA Ops:
  0.6 96.1 %shard_map.93 = (f32[32,8,256]{2,1,0:T(8,128)}, f32[32,8,256]{2,1,0:T(8,128)}, f32[32,8,256]{2,1,0:T(8,128)}, bf16[256,256]{1,0:T(8,128)(2,1)}) custom-call(bf16[1024,1024]{1,0:T(8,128)(2,1)} %acts_hbm.1, bf16[1024,256]{1,0:T(8,128)(2,1)} %bitcast.2, f32[256,1,256]{2,1,0:T(1,128)} %mas_hbm.1, f32[256,1,256]{2,1,0:T(1,128)} %fir_hbm.1, ...), custom_call_target="tpu_custom_call" | custom-call | flops 5368709120 | bytes 8388608 | tf_op jit(solution)/shard_map/pallas_call | solution.py:493
  96.8 2.1 %shard_map.94 = (f32[32,8,256]{2,1,0:T(8,128)}, f32[32,8,256]{2,1,0:T(8,128)}, f32[32,8,256]{2,1,0:T(8,128)}, bf16[256,256]{1,0:T(8,128)(2,1)}) custom-call(f32[32,8,256]{2,1,0:T(8,128)} %get-tuple-element.12.a_ref, f32[32,8,256]{2,1,0:T(8,128)} %get-tuple-element.13.b_ref, f32[32,8,256]{2,1,0:T(8,128)} %get-tuple-element.14.c_ref, ...), custom_call_target="tpu_custom_call" | custom-call | tf_op jit(solution)/shard_map/pallas_call | solution.py:553

commit v4 on v3

--- a/solution.py
+++ b/solution.py
@@ -148,7 +148,7 @@
     def cot_arrived(n, block):
         cot_copy(n, block, xn).wait_recv()
 
-    def product(j):
+    def product_for_sib(j):
         def tile(i, carry):
             rows = pl.multiple_of((1 - k) * HALF + i * 256, 256)
             pair_out[j, pl.ds(pl.multiple_of(i * 256, 256), 256), :] = jnp.dot(
@@ -159,14 +159,19 @@
         lax.fori_loop(0, HALF // 256, tile, 0)
         go(remote(pair_out.at[j], pair_in.at[j], pair_send.at[j], pair_recv.at[j], sib))
 
-        def mine(i, carry):
+    def product_to_keep(j):
+        def tile(i, carry):
             rows = pl.multiple_of(k * HALF + i * 256, 256)
             prod[j, pl.ds(pl.multiple_of(i * 256, 256), 256), :] = jnp.dot(
                 acts_t[pl.ds(rows, 256), :], cots[head[j]], preferred_element_type=F32
             )
             return carry
 
-        lax.fori_loop(0, HALF // 256, mine, 0)
+        lax.fori_loop(0, HALF // 256, tile, 0)
+
+    def product(j):
+        product_for_sib(j)
+        product_to_keep(j)
 
     def pair_arrived(j):
         remote(pair_out.at[j], pair_in.at[j], pair_send.at[j], pair_recv.at[j], sib).wait_recv()
@@ -224,6 +229,105 @@
             go(remote(*final_args(j)[1:]))
         else:
             go_or_keep(*final_args(0))
+
+    place, across = xh * NZ + z, (1 - xh) * NZ + z
+    half_rows = pl.ds(pl.multiple_of(k * CH, CH), CH)
+    other_rows = pl.ds(pl.multiple_of((1 - k) * CH, CH), CH)
+    column = (xl, 1 - xl)
+
+    def view(at, p, u=None, rows=half_rows):
+        if u is None:
+            return w_all.at[at, :, column[p], rows, :]
+        return w_all.at[at, u, column[p], rows, :]
+
+    def units(p, s=0, r=0):
+        if s == 3:
+            return (r,)
+        return (None,) if p == 0 else (0, 1)
+
+    def slot_of(u):
+        return 0 if u is None else u
+
+    def x_copy(at, p, u):
+        ref = view(at, p, u)
+        return remote(ref, ref, x_send.at[p, slot_of(u)], x_recv.at[p, slot_of(u)], xpart)
+
+    def block_of(stream, r, s):
+        at = (z + NZ - 1 - s) % NZ if r == 0 else (z + 1 + s) % NZ
+        return (xh if stream == 0 else 1 - xh) * NZ + at
+
+    def round_copy(ref, p, stream, r, s, u):
+        n = (p, stream, r, s, slot_of(u))
+        return remote(ref, ref, wr_send.at[n], wr_recv.at[n], (dev_up, dev_down)[r])
+
+    def send_on(p, stream, r, s, u):
+        go(round_copy(view(block_of(stream, r, s - 1), p, u), p, stream, r, s, u))
+
+    def sib_copy(p, n, ref):
+        return remote(ref, ref, sib_send.at[p, n], sib_recv.at[p, n], sib)
+
+    def add(at, p):
+        value = acc[...]
+        for u in range(2):
+            source = (at // NZ) * 4 + 2 * u + column[p]
+            cols = source * FEAT + (at % NZ) * 2 * CH
+            value += jnp.dot(
+                long_v[:, pl.ds(pl.multiple_of(cols, 2 * CH), 2 * CH)],
+                w_all[at, u, column[p]],
+                preferred_element_type=F32,
+            )
+        acc[...] = value
+
+    pending = []
+
+    def catch_up(entries):
+        for p, n, at, u, last in pending:
+            sib_copy(p, n, view(at, p, u, other_rows)).wait_recv()
+            if last:
+                add(at, p)
+        pending[:] = entries
+
+    def make_weights(p):
+        for u in range(2):
+            q = 2 * u + column[p]
+            for a in range(2):
+                remote(
+                    fin.at[0], land.at[a, q], fin_send.at[0], land_recv.at[a, q], xn
+                ).wait_recv()
+            grad = (land[0, q].astype(F32) + land[1, q].astype(F32)).astype(BF16)
+            grad_out[q] = grad
+            w_all[place, u, column[p], half_rows, :] = adamw(
+                lent[q, 0], lent[q, 1], lent[q, 2], grad.astype(F32)
+            )[0].astype(BF16)
+        for u in units(p):
+            go(x_copy(place, p, u))
+            for r in range(2):
+                send_on(p, 0, r, 0, u)
+        go(sib_copy(p, 0, view(place, p)))
+
+    def crossed(p):
+        for u in units(p):
+            x_copy(across, p, u).wait_recv()
+            for r in range(2):
+                send_on(p, 1, r, 0, u)
+        go(sib_copy(p, 1, view(across, p)))
+        catch_up([(p, 0, place, None, True), (p, 1, across, None, True)])
+
+    def step(p, stream, s):
+        come = []
+        for r in range(2):
+            at = block_of(stream, r, s)
+            for u in units(p, s, r):
+                round_copy(view(at, p, u), p, stream, r, s, u).wait_recv()
+                if s < 2:
+                    send_on(p, stream, r, s + 1, u)
+                elif s == 2 and (u is None or u == r):
+                    send_on(p, stream, r, 3, r)
+            n = 2 + stream * 8 + s * 2 + r
+            u = None if s < 3 else r
+            go(sib_copy(p, n, view(at, p, u)))
+            come.append((p, n, at, u, s < 3 or r == 1))
+        catch_up(come)
 
     loads[0].wait()
     def half(j, side):
@@ -291,83 +395,40 @@
         for j in range(4):
             ring(j, s)
         ring(4, s - 1)
-    for j in range(5, 8):
-        for side in range(2):
-            cot_arrived(2 * j - 2 + side, half(j, side))
-        product(j)
-    for j in range(5, 8):
-        pair_arrived(j)
-        ring(j, 0)
-    ring(4, 3)
-    for j in range(4):
-        finish(j)
-    for j in range(5, 8):
-        ring(j, 1)
-    finish(4)
-    for s in range(2, 4):
-        for j in range(5, 8):
-            ring(j, s)
-    for j in range(5, 8):
-        finish(j)
-
-    place = xh * NZ + z
-    half_rows = pl.ds(pl.multiple_of(k * CH, CH), CH)
     for q in range(4):
         remote(
             state.at[:, pl.ds(0, CH), :], lent.at[q], pre_send.at[0], pre_recv.at[q], xn
         ).wait_recv()
-    for q in range(4):
-        for a in range(2):
-            remote(
-                fin.at[0], land.at[a, q], fin_send.at[0], land_recv.at[a, q], xn
-            ).wait_recv()
-        grad = (land[0, q].astype(F32) + land[1, q].astype(F32)).astype(BF16)
-        grad_out[q] = grad
-        w_all[place, q, half_rows, :] = adamw(
-            lent[q, 0], lent[q, 1], lent[q, 2], grad.astype(F32)
-        )[0].astype(BF16)
-
-    other_rows = pl.ds(pl.multiple_of((1 - k) * CH, CH), CH)
-
-    def view(at, p, rows=half_rows):
-        return w_all.at[at, pl.ds(2 * p, 2), rows, :]
-
-    def x_copy(at, p):
-        return remote(view(at, p), view(at, p), x_send.at[p], x_recv.at[p], xpart)
-
-    def block_of(stream, r, s):
-        at = (z + NZ - 1 - s) % NZ if r == 0 else (z + 1 + s) % NZ
-        return (xh if stream == 0 else 1 - xh) * NZ + at
-
-    def halves(r, s):
-        return range(2) if s < 3 else (r,)
-
-    def weights_copy(stream, r, s, p):
-        src = view(block_of(stream, r, s - 1), p)
-        return remote(
-            src, src, wr_send.at[stream, r, s, p], wr_recv.at[stream, r, s, p],
-            (dev_up, dev_down)[r],
-        )
-
-    def weights_arrived(stream, r, s, p):
-        dst = view(block_of(stream, r, s), p)
-        remote(
-            dst, dst, wr_send.at[stream, r, s, p], wr_recv.at[stream, r, s, p],
-            (dev_up, dev_down)[r],
-        ).wait_recv()
-
-    def to_sib(n, ref):
-        go(remote(ref, ref, sib_send.at[n], sib_recv.at[n], sib))
-
-    def sib_arrived(n, ref):
-        remote(ref, ref, sib_send.at[n], sib_recv.at[n], sib).wait_recv()
-
-    for p in range(2):
-        go(x_copy(place, p))
-        for r in range(2):
-            go(weights_copy(0, r, 0, p))
-    for p in range(2):
-        to_sib(p, view(place, p))
+    loads[5].wait()
+    acc[...] = jnp.zeros_like(acc)
+    for j in range(4):
+        finish(j)
+    ring(4, 3)
+    for j in range(5, 8):
+        for side in range(2):
+            cot_arrived(2 * j - 2 + side, half(j, side))
+        product_for_sib(j)
+    for j in range(5, 8):
+        product_to_keep(j)
+        pair_arrived(j)
+        ring(j, 0)
+    finish(4)
+    for j in range(5, 8):
+        ring(j, 1)
+    make_weights(0)
+    for j in range(5, 8):
+        ring(j, 2)
+    step(0, 0, 0)
+    crossed(0)
+    for j in range(5, 8):
+        ring(j, 3)
+    step(0, 0, 1)
+    step(0, 1, 0)
+    for j in range(5, 8):
+        finish(j)
+    step(0, 0, 2)
+    step(0, 1, 1)
+    make_weights(1)
 
     def post_args(q):
         zo, ko = owner(q)
@@ -380,32 +441,6 @@
     for q in range(4):
         go_or_keep(*post_args(q))
 
-    loads[5].wait()
-
-    def add(at, start=False):
-        value = 0.0
-        for q in range(4):
-            cols = ((at // NZ) * 4 + q) * FEAT + (at % NZ) * 2 * CH
-            value += jnp.dot(
-                long_v[:, pl.ds(pl.multiple_of(cols, 2 * CH), 2 * CH)],
-                w_all[at, q],
-                preferred_element_type=F32,
-            )
-        if start:
-            acc[...] = value
-        else:
-            acc[...] += value
-
-    across = (1 - xh) * NZ + z
-    for p in range(2):
-        x_copy(across, p).wait_recv()
-        for r in range(2):
-            go(weights_copy(1, r, 0, p))
-        to_sib(2 + p, view(across, p))
-    for p in range(2):
-        sib_arrived(p, view(place, p, other_rows))
-    add(place, True)
-
     def state_copy(o):
         to = (m + o) % NM
         return remote(fresh.at[to], arrived.at[m], st_send.at[o], st_recv.at[o], (d, to))
@@ -414,53 +449,41 @@
         pltpu.make_async_copy(out_v.at[n], ref, out_sem.at[n])
         for n, ref in enumerate((nm_hbm, nf_hbm, ns_hbm))
     ]
-    pending = [(2, across, 0, False), (3, across, 1, True)]
-
-    def catch_up():
-        for n, at, p, last in pending:
-            sib_arrived(n, view(at, p, other_rows))
-            if last:
-                add(at)
-
-    for s in range(4):
-        for stream in range(2):
-            come = []
-            for r in range(2):
-                for p in halves(r, s):
-                    weights_arrived(stream, r, s, p)
-                    if s < 2 or (s == 2 and p == r):
-                        go(weights_copy(stream, r, s + 1, p))
-                    n = 4 + stream * 16 + s * 4 + r * 2 + p
-                    at = block_of(stream, r, s)
-                    to_sib(n, view(at, p))
-                    come.append((n, at, p, p == 1))
-            catch_up()
-            pending = come
-        if s == 0:
-            for n in range(4):
-                remote(
-                    grad_out.at[0], grad_in.at[n], post_send.at[0], post_recv.at[n], xn
-                ).wait_recv()
-                rows = pl.ds(n * CH, CH)
-                new = adamw(
-                    state[0, rows, :], state[1, rows, :], state[2, rows, :], grad_in[n].astype(F32)
-                )
-                for a, value in enumerate(new):
-                    fresh[2 * n, a] = value[: CH // 2]
-                    fresh[2 * n + 1, a] = value[CH // 2 :]
-            for o in range(1, NM):
-                go(state_copy(o))
-        if s == 2:
-            for a in range(3):
-                arrived[m, a] = fresh[m, a]
-            for o in range(1, NM):
-                at = (m + NM - o) % NM
-                remote(fresh.at[m], arrived.at[at], st_send.at[o], st_recv.at[o], xn).wait_recv()
-            for a in range(3):
-                for h in range(NM):
-                    out_v[a, :, h, :] = arrived[h, a]
-                outs[a].start()
-    catch_up()
+    step(0, 0, 3)
+    step(0, 1, 2)
+    step(1, 0, 0)
+    crossed(1)
+    for n in range(4):
+        remote(
+            grad_out.at[0], grad_in.at[n], post_send.at[0], post_recv.at[n], xn
+        ).wait_recv()
+        rows = pl.ds(n * CH, CH)
+        new = adamw(
+            state[0, rows, :], state[1, rows, :], state[2, rows, :], grad_in[n].astype(F32)
+        )
+        for a, value in enumerate(new):
+            fresh[2 * n, a] = value[: CH // 2]
+            fresh[2 * n + 1, a] = value[CH // 2 :]
+    for o in range(1, NM):
+        go(state_copy(o))
+    step(0, 1, 3)
+    step(1, 0, 1)
+    step(1, 1, 0)
+    step(1, 0, 2)
+    step(1, 1, 1)
+    step(1, 0, 3)
+    step(1, 1, 2)
+    for a in range(3):
+        arrived[m, a] = fresh[m, a]
+    for o in range(1, NM):
+        at = (m + NM - o) % NM
+        remote(fresh.at[m], arrived.at[at], st_send.at[o], st_recv.at[o], xn).wait_recv()
+    for a in range(3):
+        for h in range(NM):
+            out_v[a, :, h, :] = arrived[h, a]
+        outs[a].start()
+    step(1, 1, 3)
+    catch_up([])
     kv_v[...] = acc[...].astype(BF16)
     kv_out = pltpu.make_async_copy(kv_v, kv_hbm, out_sem.at[3])
     kv_out.start()
@@ -514,7 +537,7 @@
             pltpu.VMEM((NM, 3, ROWS // NM, COL), F32),
             pltpu.VMEM((NM, 3, ROWS // NM, COL), F32),
             pltpu.VMEM((3, ROWS // NM, NM, COL), F32),
-            pltpu.VMEM((ND // 2, 4, 2 * CH, COL), BF16),
+            pltpu.VMEM((ND // 2, 2, 2, 2 * CH, COL), BF16),
             pltpu.VMEM((ROWS, ND * ROWS), BF16),
             pltpu.VMEM((ROWS, COL), F32),
             pltpu.VMEM((ROWS, COL), BF16),
@@ -534,12 +557,12 @@
             dma((4,)),
             dma((NM,)),
             dma((NM,)),
-            dma((2,)),
-            dma((2,)),
-            dma((2, 2, 4, 2)),
-            dma((2, 2, 4, 2)),
-            dma((36,)),
-            dma((36,)),
+            dma((2, 2)),
+            dma((2, 2)),
+            dma((2, 2, 2, 4, 2)),
+            dma((2, 2, 2, 4, 2)),
+            dma((2, 18)),
+            dma((2, 18)),
         ],
         compiler_params=pltpu.CompilerParams(
             collective_id=0, has_side_effects=True, vmem_limit_bytes=56 * 1024 * 1024

time: 99.3 us -> 101 us (1.017)
  Pallas kernels: 98.2 us -> 99.8 us
    pallas_call x1, Pallas kernels: 96.1 us -> 97.7 us  [on_device(): pl.pallas_call(kernel, out_shape=out_shape, in_specs=[anywhere] * 6, out_...]
where the time goes in v4:
time: 101 us; the launch traced here: 100 us
  Pallas kernels  99.8 us (99%)
    pallas_call x1, Pallas kernels, on_device(): pl.pallas_call(kernel, out_shape=out_shape, in_specs=[anywhere] * 6, out_...  97.7 us
    pallas_call x1, Pallas kernels, on_device(): pl.pallas_call(settle, out_shape=out_shape, in_specs=[pl.BlockSpec(memory...  2.09 us

profile of v4, /device:TPU:1, one launch (start us, length us, event | category | flops | bytes accessed | tf_op | source)
XLA Modules:
  0.0 100.5 jit_solution(15545791939748523618)
XLA Ops:
  0.6 97.7 %shard_map.93 = (f32[32,8,256]{2,1,0:T(8,128)}, f32[32,8,256]{2,1,0:T(8,128)}, f32[32,8,256]{2,1,0:T(8,128)}, bf16[256,256]{1,0:T(8,128)(2,1)}) custom-call(bf16[1024,1024]{1,0:T(8,128)(2,1)} %acts_hbm.1, bf16[1024,256]{1,0:T(8,128)(2,1)} %bitcast.2, f32[256,1,256]{2,1,0:T(1,128)} %mas_hbm.1, f32[256,1,256]{2,1,0:T(1,128)} %fir_hbm.1, ...), custom_call_target="tpu_custom_call" | custom-call | flops 5368709120 | bytes 8388608 | tf_op jit(solution)/shard_map/pallas_call | solution.py:516
  98.4 2.1 %shard_map.94 = (f32[32,8,256]{2,1,0:T(8,128)}, f32[32,8,256]{2,1,0:T(8,128)}, f32[32,8,256]{2,1,0:T(8,128)}, bf16[256,256]{1,0:T(8,128)(2,1)}) custom-call(f32[32,8,256]{2,1,0:T(8,128)} %get-tuple-element.12.a_ref, f32[32,8,256]{2,1,0:T(8,128)} %get-tuple-element.13.b_ref, f32[32,8,256]{2,1,0:T(8,128)} %get-tuple-element.14.c_ref, ...), custom_call_target="tpu_custom_call" | custom-call | tf_op jit(solution)/shard_map/pallas_call | solution.py:576

commit v5 on v4

--- a/solution.py
+++ b/solution.py
@@ -232,62 +232,9 @@
 
     place, across = xh * NZ + z, (1 - xh) * NZ + z
     half_rows = pl.ds(pl.multiple_of(k * CH, CH), CH)
-    other_rows = pl.ds(pl.multiple_of((1 - k) * CH, CH), CH)
     column = (xl, 1 - xl)
 
-    def view(at, p, u=None, rows=half_rows):
-        if u is None:
-            return w_all.at[at, :, column[p], rows, :]
-        return w_all.at[at, u, column[p], rows, :]
-
-    def units(p, s=0, r=0):
-        if s == 3:
-            return (r,)
-        return (None,) if p == 0 else (0, 1)
-
-    def slot_of(u):
-        return 0 if u is None else u
-
-    def x_copy(at, p, u):
-        ref = view(at, p, u)
-        return remote(ref, ref, x_send.at[p, slot_of(u)], x_recv.at[p, slot_of(u)], xpart)
-
-    def block_of(stream, r, s):
-        at = (z + NZ - 1 - s) % NZ if r == 0 else (z + 1 + s) % NZ
-        return (xh if stream == 0 else 1 - xh) * NZ + at
-
-    def round_copy(ref, p, stream, r, s, u):
-        n = (p, stream, r, s, slot_of(u))
-        return remote(ref, ref, wr_send.at[n], wr_recv.at[n], (dev_up, dev_down)[r])
-
-    def send_on(p, stream, r, s, u):
-        go(round_copy(view(block_of(stream, r, s - 1), p, u), p, stream, r, s, u))
-
-    def sib_copy(p, n, ref):
-        return remote(ref, ref, sib_send.at[p, n], sib_recv.at[p, n], sib)
-
-    def add(at, p):
-        value = acc[...]
-        for u in range(2):
-            source = (at // NZ) * 4 + 2 * u + column[p]
-            cols = source * FEAT + (at % NZ) * 2 * CH
-            value += jnp.dot(
-                long_v[:, pl.ds(pl.multiple_of(cols, 2 * CH), 2 * CH)],
-                w_all[at, u, column[p]],
-                preferred_element_type=F32,
-            )
-        acc[...] = value
-
-    pending = []
-
-    def catch_up(entries):
-        for p, n, at, u, last in pending:
-            sib_copy(p, n, view(at, p, u, other_rows)).wait_recv()
-            if last:
-                add(at, p)
-        pending[:] = entries
-
-    def make_weights(p):
+    def put_together(p):
         for u in range(2):
             q = 2 * u + column[p]
             for a in range(2):
@@ -299,35 +246,50 @@
             w_all[place, u, column[p], half_rows, :] = adamw(
                 lent[q, 0], lent[q, 1], lent[q, 2], grad.astype(F32)
             )[0].astype(BF16)
-        for u in units(p):
-            go(x_copy(place, p, u))
-            for r in range(2):
-                send_on(p, 0, r, 0, u)
-        go(sib_copy(p, 0, view(place, p)))
-
-    def crossed(p):
-        for u in units(p):
-            x_copy(across, p, u).wait_recv()
-            for r in range(2):
-                send_on(p, 1, r, 0, u)
-        go(sib_copy(p, 1, view(across, p)))
-        catch_up([(p, 0, place, None, True), (p, 1, across, None, True)])
-
-    def step(p, stream, s):
-        come = []
-        for r in range(2):
-            at = block_of(stream, r, s)
-            for u in units(p, s, r):
-                round_copy(view(at, p, u), p, stream, r, s, u).wait_recv()
-                if s < 2:
-                    send_on(p, stream, r, s + 1, u)
-                elif s == 2 and (u is None or u == r):
-                    send_on(p, stream, r, 3, r)
-            n = 2 + stream * 8 + s * 2 + r
-            u = None if s < 3 else r
-            go(sib_copy(p, n, view(at, p, u)))
-            come.append((p, n, at, u, s < 3 or r == 1))
-        catch_up(come)
+
+    def post_args(q):
+        zo, ko = owner(q)
+        slot = 2 * (z % 2) + k
+        return (
+            (zo == z) & (ko == k), grad_out.at[q], grad_in.at[slot],
+            post_send.at[q], post_recv.at[slot], (dp_index(xh, zo, ko), m),
+        )
+
+    def post(p):
+        for u in range(2):
+            go_or_keep(*post_args(2 * u + column[p]))
+
+    other_rows = pl.ds(pl.multiple_of((1 - k) * CH, CH), CH)
+
+    def view(at, p, rows=half_rows):
+        return w_all.at[at, :, column[p], rows, :]
+
+    def x_copy(at, p):
+        return remote(view(at, p), view(at, p), x_send.at[p], x_recv.at[p], xpart)
+
+    def block_of(stream, r, s):
+        at = (z + NZ - 1 - s) % NZ if r == 0 else (z + 1 + s) % NZ
+        return (xh if stream == 0 else 1 - xh) * NZ + at
+
+    def weights_copy(stream, r, s, p):
+        src = view(block_of(stream, r, s - 1), p)
+        return remote(
+            src, src, wr_send.at[stream, r, s, p], wr_recv.at[stream, r, s, p],
+            (dev_up, dev_down)[r],
+        )
+
+    def weights_arrived(stream, r, s, p):
+        dst = view(block_of(stream, r, s), p)
+        remote(
+            dst, dst, wr_send.at[stream, r, s, p], wr_recv.at[stream, r, s, p],
+            (dev_up, dev_down)[r],
+        ).wait_recv()
+
+    def to_sib(n, ref):
+        go(remote(ref, ref, sib_send.at[n], sib_recv.at[n], sib))
+
+    def sib_arrived(n, ref):
+        remote(ref, ref, sib_send.at[n], sib_recv.at[n], sib).wait_recv()
 
     loads[0].wait()
     def half(j, side):
@@ -395,51 +357,62 @@
         for j in range(4):
             ring(j, s)
         ring(4, s - 1)
-    for q in range(4):
-        remote(
-            state.at[:, pl.ds(0, CH), :], lent.at[q], pre_send.at[0], pre_recv.at[q], xn
-        ).wait_recv()
-    loads[5].wait()
-    acc[...] = jnp.zeros_like(acc)
-    for j in range(4):
-        finish(j)
-    ring(4, 3)
     for j in range(5, 8):
         for side in range(2):
             cot_arrived(2 * j - 2 + side, half(j, side))
         product_for_sib(j)
     for j in range(5, 8):
         product_to_keep(j)
+    for j in range(5, 8):
         pair_arrived(j)
         ring(j, 0)
-    finish(4)
+    ring(4, 3)
+    for j in range(4):
+        finish(j)
     for j in range(5, 8):
         ring(j, 1)
-    make_weights(0)
-    for j in range(5, 8):
-        ring(j, 2)
-    step(0, 0, 0)
-    crossed(0)
-    for j in range(5, 8):
-        ring(j, 3)
-    step(0, 0, 1)
-    step(0, 1, 0)
+    finish(4)
+    for s in range(2, 4):
+        for j in range(5, 8):
+            ring(j, s)
+    for q in range(4):
+        remote(
+            state.at[:, pl.ds(0, CH), :], lent.at[q], pre_send.at[0], pre_recv.at[q], xn
+        ).wait_recv()
+    put_together(0)
+    go(x_copy(place, 0))
+    for r in range(2):
+        go(weights_copy(0, r, 0, 0))
+    post(0)
     for j in range(5, 8):
         finish(j)
-    step(0, 0, 2)
-    step(0, 1, 1)
-    make_weights(1)
-
-    def post_args(q):
-        zo, ko = owner(q)
-        slot = 2 * (z % 2) + k
-        return (
-            (zo == z) & (ko == k), grad_out.at[q], grad_in.at[slot],
-            post_send.at[q], post_recv.at[slot], (dp_index(xh, zo, ko), m),
-        )
-
-    for q in range(4):
-        go_or_keep(*post_args(q))
+    x_copy(across, 0).wait_recv()
+    for r in range(2):
+        go(weights_copy(1, r, 0, 0))
+    put_together(1)
+    go(x_copy(place, 1))
+    for r in range(2):
+        go(weights_copy(0, r, 0, 1))
+    for p in range(2):
+        to_sib(p, view(place, p))
+    to_sib(2, view(across, 0))
+
+    post(1)
+    loads[5].wait()
+
+    def add(at, start=False):
+        value = 0.0
+        for q in range(4):
+            cols = ((at // NZ) * 4 + q) * FEAT + (at % NZ) * 2 * CH
+            value += jnp.dot(
+                long_v[:, pl.ds(pl.multiple_of(cols, 2 * CH), 2 * CH)],
+                w_all[at, q // 2, q % 2],
+                preferred_element_type=F32,
+            )
+        if start:
+            acc[...] = value
+        else:
+            acc[...] += value
 
     def state_copy(o):
         to = (m + o) % NM
@@ -449,10 +422,41 @@
         pltpu.make_async_copy(out_v.at[n], ref, out_sem.at[n])
         for n, ref in enumerate((nm_hbm, nf_hbm, ns_hbm))
     ]
-    step(0, 0, 3)
-    step(0, 1, 2)
+    pending = [(2, across, 0, False)]
+
+    def catch_up(entries):
+        for n, at, p, last in pending:
+            sib_arrived(n, view(at, p, other_rows))
+            if last:
+                add(at)
+        pending[:] = entries
+
+    def step(p, stream, s):
+        come = []
+        for r in range(2) if s < 3 else (p,):
+            weights_arrived(stream, r, s, p)
+            if s < 2 or (s == 2 and p == r):
+                go(weights_copy(stream, r, s + 1, p))
+            n = 4 + stream * 16 + s * 4 + r * 2 + p
+            at = block_of(stream, r, s)
+            to_sib(n, view(at, p))
+            come.append((n, at, p, p == 1))
+        catch_up(come)
+
+    step(0, 0, 0)
+    step(0, 1, 0)
+    x_copy(across, 1).wait_recv()
+    for r in range(2):
+        go(weights_copy(1, r, 0, 1))
+    to_sib(3, view(across, 1))
+    for p in range(2):
+        sib_arrived(p, view(place, p, other_rows))
+    add(place, True)
+    pending.append((3, across, 1, True))
     step(1, 0, 0)
-    crossed(1)
+    step(0, 0, 1)
+    step(0, 1, 1)
+    step(1, 1, 0)
     for n in range(4):
         remote(
             grad_out.at[0], grad_in.at[n], post_send.at[0], post_recv.at[n], xn
@@ -466,12 +470,13 @@
             fresh[2 * n + 1, a] = value[CH // 2 :]
     for o in range(1, NM):
         go(state_copy(o))
+    step(1, 0, 1)
+    step(0, 0, 2)
+    step(0, 1, 2)
+    step(1, 1, 1)
+    step(1, 0, 2)
+    step(0, 0, 3)
     step(0, 1, 3)
-    step(1, 0, 1)
-    step(1, 1, 0)
-    step(1, 0, 2)
-    step(1, 1, 1)
-    step(1, 0, 3)
     step(1, 1, 2)
     for a in range(3):
         arrived[m, a] = fresh[m, a]
@@ -482,6 +487,7 @@
         for h in range(NM):
             out_v[a, :, h, :] = arrived[h, a]
         outs[a].start()
+    step(1, 0, 3)
     step(1, 1, 3)
     catch_up([])
     kv_v[...] = acc[...].astype(BF16)
@@ -557,12 +563,12 @@
             dma((4,)),
             dma((NM,)),
             dma((NM,)),
-            dma((2, 2)),
-            dma((2, 2)),
-            dma((2, 2, 2, 4, 2)),
-            dma((2, 2, 2, 4, 2)),
-            dma((2, 18)),
-            dma((2, 18)),
+            dma((2,)),
+            dma((2,)),
+            dma((2, 2, 4, 2)),
+            dma((2, 2, 4, 2)),
+            dma((36,)),
+            dma((36,)),
         ],
         compiler_params=pltpu.CompilerParams(
             collective_id=0, has_side_effects=True, vmem_limit_bytes=56 * 1024 * 1024

time: 101 us -> 98.7 us (0.977)
  Pallas kernels: 99.8 us -> 98 us
    pallas_call x1, Pallas kernels: 97.7 us -> 95.9 us  [on_device(): pl.pallas_call(kernel, out_shape=out_shape, in_specs=[anywhere] * 6, out_...]
where the time goes in v5:
time: 98.7 us; the launch traced here: 98.6 us
  Pallas kernels  98 us (99%)
    pallas_call x1, Pallas kernels, on_device(): pl.pallas_call(kernel, out_shape=out_shape, in_specs=[anywhere] * 6, out_...  95.9 us
    pallas_call x1, Pallas kernels, on_device(): pl.pallas_call(settle, out_shape=out_shape, in_specs=[pl.BlockSpec(memory...  2.09 us

profile of v5, /device:TPU:1, one launch (start us, length us, event | category | flops | bytes accessed | tf_op | source)
XLA Modules:
  0.0 98.6 jit_solution(5029593998046296538)
XLA Ops:
  0.6 95.9 %shard_map.93 = (f32[32,8,256]{2,1,0:T(8,128)}, f32[32,8,256]{2,1,0:T(8,128)}, f32[32,8,256]{2,1,0:T(8,128)}, bf16[256,256]{1,0:T(8,128)(2,1)}) custom-call(bf16[1024,1024]{1,0:T(8,128)(2,1)} %acts_hbm.1, bf16[1024,256]{1,0:T(8,128)(2,1)} %bitcast.2, f32[256,1,256]{2,1,0:T(1,128)} %mas_hbm.1, f32[256,1,256]{2,1,0:T(1,128)} %fir_hbm.1, ...), custom_call_target="tpu_custom_call" | custom-call | flops 5368709120 | bytes 8388608 | tf_op jit(solution)/shard_map/pallas_call | solution.py:522
  96.5 2.1 %shard_map.94 = (f32[32,8,256]{2,1,0:T(8,128)}, f32[32,8,256]{2,1,0:T(8,128)}, f32[32,8,256]{2,1,0:T(8,128)}, bf16[256,256]{1,0:T(8,128)(2,1)}) custom-call(f32[32,8,256]{2,1,0:T(8,128)} %get-tuple-element.12.a_ref, f32[32,8,256]{2,1,0:T(8,128)} %get-tuple-element.13.b_ref, f32[32,8,256]{2,1,0:T(8,128)} %get-tuple-element.14.c_ref, ...), custom_call_target="tpu_custom_call" | custom-call | tf_op jit(solution)/shard_map/pallas_call | solution.py:582
